TPU v7x, 128 devices: a whole 4x4x4 slice. The times are simulated.
128 devices in a mesh: tm: 8 (over x, z_lo), space: 16 (over y, z_hi, core).
Axes of the slice: x: 4, y: 4, z: 4 (z_hi: 2, z_lo: 2; z = z_hi * 2 + z_lo), core: 2. Of those that a mesh axis runs over, the one named last changes fastest.
Arguments:
- flow_state: float32 [16, 4, 64, 64, 128], P('tm', None, 'space'), may hold values from -6 to 6
- adjoint_state: float32 [16, 4, 64, 64, 128], P('tm', None, 'space'), may hold values from -6 to 6
- density: float32 [64, 64, 128], P('space'), may hold values from 0 to 1
- design_mask: int32 [64, 64, 128], P('space'), may hold values 0 or 1
- labels: int32 [64, 64, 128], P('space'), may hold values from 0 to 2
Outputs:
- flow_residual: float32 [16, 4, 64, 64, 128], P('tm', None, 'space')
- adjoint_residual: float32 [16, 4, 64, 64, 128], P('tm', None, 'space')
All inputs are finite; a program needn't handle non-finite values. No bound on the sum of `design_mask` on one device may be relied on, other than what follows from the above.
Results may differ from a plain program's by a relative error of at most 0.0001.
Values sent between devices are 32-bit elements; how exact they have to be, the bound alone decides.
No kernel may reach another device: no remote copies, remote signals or barrier semaphores. Data moves between devices by JAX's collectives and lax.ppermute only.
A program may use at most 256 MiB of HBM per device.

v0:
```python
import jax
import jax.numpy as jnp
from jax import lax
from jax.experimental import pallas as pl
from jax.experimental.pallas import tpu as pltpu
from jax.sharding import PartitionSpec as P
import numpy as np

NT = 16
NU_INF = 0.0616
NU_ZERO = 1.0
LAMBDA_SQ = 3.313 * 3.313
POWER = (0.3568 - 1.0) / 2.0
BRINKMAN_MAX = 8.0
RAMP_SHAPE = 0.1
TIME_SCALE = 0.25

PLANES = 4
ROWS = 64
LANES = 128
TOP = 8
PADDED = ROWS + 2 * TOP

MU_A = 0.25 * NU_INF
MU_B = 0.25 * (NU_ZERO - NU_INF)
SHEAR = LAMBDA_SQ / 8.0
DMU = (NU_ZERO - NU_INF) * POWER * LAMBDA_SQ / 16.0


def viscosity(square_sum):
    q = 1.0 + SHEAR * square_sum
    log_q = jnp.log(q)
    return MU_A + MU_B * jnp.exp(POWER * log_q), DMU * jnp.exp((POWER - 1.0) * log_q)


def outer_cell(u, lam, axis):
    strain = [u[j] + u[j] if j == axis else u[j] for j in range(3)]
    rate = [lam[j] + lam[j] if j == axis else lam[j] for j in range(3)]
    others = [j for j in range(3) if j != axis]
    square = sum(strain[j] * strain[j] for j in others)
    cross = sum(strain[j] * rate[j] for j in others)
    square = square + square + strain[axis] * strain[axis]
    cross = cross + cross + strain[axis] * rate[axis]
    mu, dmu = viscosity(square)
    slope = dmu * cross
    return [mu * s for s in strain], [mu * e + slope * s for s, e in zip(strain, rate)]


def stencil_kernel(
    inflow_ref, flow_ref, adj_ref, low_ref, high_ref, density_ref, mask_ref, labels_ref,
    out_f, out_a, w, tx, fx, ty, fy, sems,
):
    insts = out_f.shape[0]
    rows = pl.ds(TOP, ROWS)
    copies = []
    for source, base, last in ((flow_ref, 0, 6), (adj_ref, 3, 7)):
        copies.append((source.at[:, 0:3], w.at[:, base : base + 3, 2:6, rows, :]))
        copies.append((source.at[:, 3], w.at[:, last, 2:6, rows, :]))
    for source, first in ((low_ref, 0), (high_ref, 6)):
        for c in range(6):
            copies.append((source.at[:, 2 * c : 2 * c + 2], w.at[:, c, first : first + 2, rows, :]))
        near = 1 if first == 0 else 6
        copies.append((source.at[:, 12:14], w.at[:, 6:8, near, rows, :]))
    handles = [pltpu.make_async_copy(a, b, sems.at[i]) for i, (a, b) in enumerate(copies)]
    for h in handles:
        h.start()
    zero = jnp.zeros((TOP, LANES), jnp.float32)

    def clear(i, _):
        for c in range(6):
            for p in range(8):
                w[i, c, p, 0:TOP, :] = zero
                w[i, c, p, TOP + ROWS : PADDED, :] = zero
        return 0

    lax.fori_loop(0, insts, clear, 0)
    for h in handles:
        h.wait()

    lane = lax.broadcasted_iota(jnp.int32, (8, LANES), 1)
    is_first = lane == 0
    is_last = lane == LANES - 1

    def along_z(f):
        up = jnp.where(is_last, 0.0, pltpu.roll(f, LANES - 1, 1))
        down = jnp.where(is_first, 0.0, pltpu.roll(f, 1, 1))
        return up - down

    def along_z_outer(f, outer):
        up = jnp.where(is_last, -outer, pltpu.roll(f, LANES - 1, 1))
        down = jnp.where(is_first, outer, pltpu.roll(f, 1, 1))
        return up - down

    def tile_work(i, p, t, interior):
        r = TOP + pl.multiple_of(t * 8, 8)
        here = pl.ds(r, 8)
        u = [w[i, j, p, here, :] for j in range(3)]
        lam = [w[i, 3 + j, p, here, :] for j in range(3)]
        grads, rates = [], []
        for base, values, into in ((0, u, grads), (3, lam, rates)):
            into.append([w[i, base + j, p + 1, here, :] - w[i, base + j, p - 1, here, :] for j in range(3)])
            into.append(
                [w[i, base + j, p, pl.ds(r + 1, 8), :] - w[i, base + j, p, pl.ds(r - 1, 8), :] for j in range(3)]
            )
            into.append([along_z(v) for v in values])
        strain = [[grads[k][j] + grads[j][k] for k in range(3)] for j in range(3)]
        rate = [[rates[k][j] + rates[j][k] for k in range(3)] for j in range(3)]
        pairs = ((0, 1), (0, 2), (1, 2))
        square = sum(strain[j][k] * strain[j][k] for j, k in pairs)
        cross = sum(strain[j][k] * rate[j][k] for j, k in pairs)
        square = square + square + sum(strain[j][j] * strain[j][j] for j in range(3))
        cross = cross + cross + sum(strain[j][j] * rate[j][j] for j in range(3))
        mu, dmu = viscosity(square)
        slope = dmu * cross
        half_u = [0.5 * v for v in u]
        half_p = 0.5 * w[i, 6, p, here, :]
        half_q = 0.5 * w[i, 7, p, here, :]

        def flux(j, k):
            t_jk = mu * strain[j][k]
            f_jk = mu * rate[j][k] + slope * strain[j][k] + half_u[k] * lam[j]
            if j == k:
                t_jk, f_jk = t_jk - half_p, f_jk + half_q
            return t_jk, f_jk

        for j in range(3):
            t_jk, f_jk = flux(j, 0)
            tx[j, p, pl.ds(r - TOP, 8), :] = t_jk
            fx[j, p, pl.ds(r - TOP, 8), :] = f_jk
        if not interior:
            return
        q = p - 2
        out_rows = pl.ds(r - TOP, 8)
        for j in range(3):
            t_jk, f_jk = flux(j, 1)
            ty[j, q, here, :] = t_jk
            fy[j, q, here, :] = f_jk
        outer_t, outer_f = outer_cell(u, lam, 2)
        design = jnp.where(mask_ref[q, out_rows, :] == 1, density_ref[q, out_rows, :], 1.0)
        label = labels_ref[q, out_rows, :]
        ramp = (BRINKMAN_MAX * RAMP_SHAPE) * (1.0 - design) / (RAMP_SHAPE + design)
        penalty = jnp.where(label == 0, ramp, BRINKMAN_MAX)
        target = jnp.where(label == 2, inflow_ref[i], 0.0)
        half_lam = [0.5 * v for v in lam]
        for j in range(3):
            t_jk, f_jk = flux(j, 2)
            shifted = u[j] - target if j == 0 else u[j]
            out_f[i, j, q, out_rows, :] = (
                sum(half_u[k] * grads[k][j] for k in range(3)) - along_z_outer(t_jk, outer_t[j]) + penalty * shifted
            )
            out_a[i, j, q, out_rows, :] = (
                sum(half_lam[k] * grads[j][k] for k in range(3)) - along_z_outer(f_jk, outer_f[j]) + penalty * lam[j]
            )
        out_f[i, 3, q, out_rows, :] = 0.25 * (strain[0][0] + strain[1][1] + strain[2][2])
        out_a[i, 3, q, out_rows, :] = -0.25 * (rate[0][0] + rate[1][1] + rate[2][2])

    def y_edges(i, q):
        p = q + 2
        for first, keep, row, sign in ((TOP, 0, TOP - 1, 1.0), (TOP + ROWS - 8, 7, TOP + ROWS, -1.0)):
            u = [w[i, j, p, first : first + 8, :] for j in range(3)]
            lam = [w[i, 3 + j, p, first : first + 8, :] for j in range(3)]
            outer_t, outer_f = outer_cell(u, lam, 1)
            for j in range(3):
                ty[j, q, row : row + 1, :] = sign * outer_t[j][keep : keep + 1]
                fy[j, q, row : row + 1, :] = sign * outer_f[j][keep : keep + 1]

    def instance(i, _):
        def outer_planes(n, _):
            side, t = n // 8, n % 8
            tile_work(i, 1 + 5 * side, t, False)
            return 0

        lax.fori_loop(0, 16, outer_planes, 0)

        def inner_planes(n, _):
            tile_work(i, 2 + n // 8, n % 8, True)
            return 0

        lax.fori_loop(0, 8 * PLANES, inner_planes, 0)

        def edges(q, _):
            y_edges(i, q)
            return 0

        lax.fori_loop(0, PLANES, edges, 0)

        def collect(n, _):
            q, t = n // 8, n % 8
            r = pl.multiple_of(t * 8, 8)
            for out, x_flux, y_flux in ((out_f, tx, ty), (out_a, fx, fy)):
                for j in range(3):
                    d_x = x_flux[j, q + 3, pl.ds(r, 8), :] - x_flux[j, q + 1, pl.ds(r, 8), :]
                    d_y = y_flux[j, q, pl.ds(r + TOP + 1, 8), :] - y_flux[j, q, pl.ds(r + TOP - 1, 8), :]
                    out[i, j, q, pl.ds(r, 8), :] = out[i, j, q, pl.ds(r, 8), :] - d_x - d_y
            return 0

        lax.fori_loop(0, 8 * PLANES, collect, 0)
        return 0

    lax.fori_loop(0, insts, instance, 0)


def stencil(inflow, flow, adj, low, high, density, mask, labels):
    insts = flow.shape[0]
    shape = jax.ShapeDtypeStruct(flow.shape, jnp.float32)
    whole = pl.BlockSpec(memory_space=pltpu.VMEM)
    anywhere = pl.BlockSpec(memory_space=pl.ANY)
    return pl.pallas_call(
        stencil_kernel,
        out_shape=(shape, shape),
        in_specs=[pl.BlockSpec(memory_space=pltpu.SMEM)] + [anywhere] * 4 + [whole] * 3,
        out_specs=(whole, whole),
        scratch_shapes=[
            pltpu.VMEM((insts, 8, 8, PADDED, LANES), jnp.float32),
            pltpu.VMEM((3, 8, ROWS, LANES), jnp.float32),
            pltpu.VMEM((3, 8, ROWS, LANES), jnp.float32),
            pltpu.VMEM((3, PLANES, PADDED, LANES), jnp.float32),
            pltpu.VMEM((3, PLANES, PADDED, LANES), jnp.float32),
            pltpu.SemaphoreType.DMA((18,)),
        ],
        compiler_params=pltpu.CompilerParams(vmem_limit_bytes=40 << 20),
        cost_estimate=pl.CostEstimate(flops=40_000_000, bytes_accessed=8_000_000, transcendentals=400_000),
        name="stencil",
    )(inflow, flow, adj, low, high, density, mask, labels)


def spectral_row():
    k = np.arange(1, 8)
    return [float(v) for v in TIME_SCALE * 0.5 * np.where(k % 2 == 0, 1.0, -1.0) / np.tan(np.pi * k / NT)]


def time_kernel(x_ref, out_ref):
    coef = spectral_row()
    comps, planes = x_ref.shape[1:3]

    def step(n, _):
        c, q = n // planes, n % planes
        x = [x_ref[m, c, q] for m in range(NT)]
        sign = jnp.where(c < comps // 2, 1.0, -1.0)
        for n0 in range(NT // 2):
            diff = [(x[(n0 - k) % NT] - x[(n0 + k) % NT]) * sign for k in range(1, 8)]
            out_ref[n0, c, q] = sum(coef[k - 1] * diff[k - 1] for k in range(1, 8))
            out_ref[n0 + 8, c, q] = -sum(coef[k - 1] * diff[7 - k] for k in range(1, 8))
        return 0

    lax.fori_loop(0, comps * planes, step, 0)


def time_derivative(x):
    return pl.pallas_call(
        time_kernel,
        out_shape=jax.ShapeDtypeStruct(x.shape, jnp.float32),
        in_specs=[pl.BlockSpec(memory_space=pltpu.VMEM)],
        out_specs=pl.BlockSpec(memory_space=pltpu.VMEM),
        compiler_params=pltpu.CompilerParams(vmem_limit_bytes=16 << 20),
        name="time_derivative",
    )(x)


def add_kernel(f_ref, a_ref, t_ref, out_f, out_a):
    blocks, insts = t_ref.shape[:2]
    for base, source, out in ((0, f_ref, out_f), (3, a_ref, out_a)):
        for i in range(insts):
            for j in range(3):
                for b in range(blocks):
                    out[i, j, :, 8 * b : 8 * b + 8, :] = source[i, j, :, 8 * b : 8 * b + 8, :] + t_ref[b, i, base + j]
            out[i, 3] = source[i, 3]


def add_time(flow_part, adj_part, time_part):
    whole = pl.BlockSpec(memory_space=pltpu.VMEM)
    shape = jax.ShapeDtypeStruct(flow_part.shape, jnp.float32)
    return pl.pallas_call(
        add_kernel,
        out_shape=(shape, shape),
        in_specs=[whole] * 3,
        out_specs=(whole, whole),
        compiler_params=pltpu.CompilerParams(vmem_limit_bytes=24 << 20),
        name="add_time",
    )(flow_part, adj_part, time_part)


def boundary(flow, adj, planes, near):
    insts = flow.shape[0]
    far = jnp.concatenate([flow[:, :3, planes], adj[:, :3, planes]], axis=1)
    last = jnp.stack([flow[:, 3, near], adj[:, 3, near]], axis=1)
    return jnp.concatenate([far.reshape(insts, 12, ROWS, LANES), last], axis=1)


def on_device(flow, adj, density, mask, labels):
    insts = flow.shape[0]
    times = lax.axis_size("tm")
    count = lax.axis_size("space")
    instances = lax.axis_index("tm") * insts + jnp.arange(insts, dtype=jnp.int32)
    inflow = 1.0 + 0.5 * jnp.sin(2.0 * jnp.pi * instances.astype(jnp.float32) / NT)

    low = lax.ppermute(
        boundary(flow, adj, slice(PLANES - 2, PLANES), PLANES - 1), "space", [(i, i + 1) for i in range(count - 1)]
    )
    high = lax.ppermute(boundary(flow, adj, slice(0, 2), 0), "space", [(i + 1, i) for i in range(count - 1)])

    both = jnp.concatenate([flow[:, :3], adj[:, :3]], axis=1)
    both = both.reshape(insts, 6, PLANES, times, ROWS // times, LANES).transpose(3, 0, 1, 2, 4, 5)
    gathered = lax.all_to_all(both, "tm", 0, 0, tiled=True)
    derived = time_derivative(gathered.reshape(NT, 6, PLANES, ROWS // times, LANES))
    derived = derived.reshape(times, insts, 6, PLANES, ROWS // times, LANES)
    time_part = lax.all_to_all(derived, "tm", 0, 0, tiled=True)

    flow_part, adj_part = stencil(inflow, flow, adj, low, high, density, mask, labels)
    return add_time(flow_part, adj_part, time_part)


def solution(mesh):
    split = P("tm", None, "space", None, None)
    cells = P("space", None, None)
    return jax.shard_map(
        on_device,
        mesh=mesh,
        in_specs=(split, split, cells, cells, cells),
        out_specs=(split, split),
        check_vma=False,
    )
```

profile of v0, /device:TPU:17, one launch (start us, length us, event | category | flops | bytes accessed | tf_op | source)
XLA Modules:
  0.0 107.3 jit_solution(8535271597642590809)
XLA Ops:
  0.6 0.0 slice-start
  0.6 0.0 slice-start.1
  0.7 1.1 %slice-done = f32[2,3,4,64,128]{4,3,2,1,0:T(8,128)S(1)} async-done(((f32[2,4,4,64,128]{4,3,2,1,0:T(8,128)}), f32[2,3,4,64,128]{4,3,2,1,0:T(8,128)S(1)}, s32[]{:S(2)}) %slice-start) | async-done | bytes 786456 | tf_op jit(solution)/shard_map/slice | solution.py:302
  1.8 0.2 slice-done.1
  2.0 1.4 %copy_bitcast_fusion = f32[8,2,6,4,8,128]{5,4,3,2,1,0:T(8,128)} fusion(f32[2,3,4,64,128]{4,3,2,1,0:T(8,128)S(1)} %slice-done.1, f32[2,3,4,64,128]{4,3,2,1,0:T(8,128)S(1)} %slice-done), kind=kLoop, calls=%fused_computation.1 | loop fusion | flops 393216 | bytes 3145728 | tf_op jit(solution)/shard_map/transpose | solution.py:303
  3.4 0.0 copy-start
  3.4 0.0 copy-start.1
  3.4 5.5 %all-to-all-start = ((f32[8,2,6,4,8,128]{5,4,3,2,1,0:T(8,128)}), f32[8,2,6,4,8,128]{5,4,3,2,1,0:T(8,128)}, u32[]{:S(2)}, u32[]{:S(2)}) async-start(f32[8,2,6,4,8,128]{5,4,3,2,1,0:T(8,128)} %copy_bitcast_fusion), calls=%async_computation | async-start | bytes 3145728 | tf_op jit(solution)/shard_map/all_to_all | solution.py:304
  8.9 0.0 copy-done
  8.9 0.8 fusion
  9.7 0.0 copy-done.1
  9.7 0.9 fusion.1
  10.6 21.4 %all-to-all-done = f32[8,2,6,4,8,128]{5,4,3,2,1,0:T(8,128)} async-done(((f32[8,2,6,4,8,128]{5,4,3,2,1,0:T(8,128)}), f32[8,2,6,4,8,128]{5,4,3,2,1,0:T(8,128)}, u32[]{:S(2)}, u32[]{:S(2)}) %all-to-all-start) | async-done | bytes 1572896 | tf_op jit(solution)/shard_map/all_to_all | solution.py:304
  32.0 2.8 %time_derivative.1 = f32[16,6,4,8,128]{4,3,2,1,0:T(8,128)S(1)} custom-call(f32[16,6,4,8,128]{4,3,2,1,0:T(8,128)} %bitcast.8.x_ref), custom_call_target="tpu_custom_call" | custom-call | tf_op jit(solution)/shard_map/time_derivative/pallas_call | solution.py:250
  34.9 0.0 copy-start.2
  34.9 1.1 %copy-done.2 = f32[16,6,4,8,128]{4,3,2,1,0:T(8,128)} copy-done((f32[16,6,4,8,128]{4,3,2,1,0:T(8,128)}, f32[16,6,4,8,128]{4,3,2,1,0:T(8,128)S(1)}, u32[]{:S(2)}) %copy-start.2) | copy-done | bytes 1572888
  36.0 4.3 %all-to-all-start.1 = ((f32[8,2,6,4,8,128]{5,4,3,2,1,0:T(8,128)}), f32[8,2,6,4,8,128]{5,4,3,2,1,0:T(8,128)}, u32[]{:S(2)}, u32[]{:S(2)}) async-start(f32[8,2,6,4,8,128]{5,4,3,2,1,0:T(8,128)} %bitcast.25), calls=%async_computation.1 | async-start | bytes 3145728 | tf_op jit(solution)/shard_map/all_to_all | solution.py:307
  40.4 1.4 %pad_maximum_fusion.2 = (f32[2,6,2,64,128]{4,3,2,1,0:T(8,128)S(1)}, f32[2,6,2,64,128]{4,3,2,1,0:T(8,128)S(1)}) fusion(f32[2,3,2,64,128]{4,3,2,1,0:T(8,128)} %get-tuple-element.9, f32[2,3,2,64,128]{4,3,2,1,0:T(8,128)} %get-tuple-element.7, f32[2,3,2,64,128]{4,3,2,1,0:T(8,128)} %get-tuple-element.8, f32[2,3,2,64,128]{4,3,2,1,0:T(8,128)S(1)} %get-tuple-element.6), kind=kLoop, calls=%fused_computation.4 | loop fusion | flops 393216 | bytes 3145728 | tf_op jit(solution)/shard_map/concatenate | solution.py:285
  41.7 0.0 copy-start.7
  41.7 0.0 copy-start.8
  41.8 0.0 copy-start.9
  41.8 1.0 pad_maximum_fusion.1
  42.8 3.5 %collective-permute-start.1 = (f32[2,14,64,128]{3,2,1,0:T(8,128)}, f32[2,14,64,128]{3,2,1,0:T(8,128)S(1)}, u32[]{:S(2)}, u32[]{:S(2)}) collective-permute-start(f32[2,14,64,128]{3,2,1,0:T(8,128)} %pad_maximum_fusion.1), channel_id=1, source_target_pairs={{1,0},{2,1},{3,2},{4,3},{5,4},{6,5},{7,6},{8,7},{9,8},{10,9},{11,1... | collective-permute-start | bytes 2752520 | tf_op jit(solution)/shard_map/ppermute | solution.py:300
  46.3 1.0 pad_maximum_fusion
  47.3 5.1 %collective-permute-start = (f32[2,14,64,128]{3,2,1,0:T(8,128)}, f32[2,14,64,128]{3,2,1,0:T(8,128)}, u32[]{:S(2)}, u32[]{:S(2)}) collective-permute-start(f32[2,14,64,128]{3,2,1,0:T(8,128)} %pad_maximum_fusion), channel_id=1, source_target_pairs={{0,1},{1,2},{2,3},{3,4},{4,5},{5,6},{6,7},{7,8},{8,9},{9,10},{10,1... | collective-permute-start | bytes 2752520 | tf_op jit(solution)/shard_map/ppermute | solution.py:297
  52.5 28.8 %collective-permute-done.1.high_ref = f32[2,14,64,128]{3,2,1,0:T(8,128)S(1)} collective-permute-done((f32[2,14,64,128]{3,2,1,0:T(8,128)}, f32[2,14,64,128]{3,2,1,0:T(8,128)S(1)}, u32[]{:S(2)}, u32[]{:S(2)}) %collective-permute-start.1) | collective-permute-done | bytes 917536 | tf_op jit(solution)/shard_map/ppermute | solution.py:300
  81.3 0.0 copy-start.5
  81.3 0.9 copy-done.5
  82.2 0.0 collective-permute-done.low_ref
  82.2 0.0 copy-done.7
  82.2 0.0 copy-done.8
  82.2 0.0 copy-done.9
  82.2 0.0 copy-start.6
  82.3 1.2 %copy-done.6 = f32[2,14,64,128]{3,2,1,0:T(8,128)S(1)} copy-done((f32[2,14,64,128]{3,2,1,0:T(8,128)S(1)}, f32[2,14,64,128]{3,2,1,0:T(8,128)}, u32[]{:S(2)}) %copy-start.6) | copy-done | bytes 917528
  83.4 18.9 %stencil.1 = (f32[2,4,4,64,128]{4,3,2,1,0:T(8,128)S(1)}, f32[2,4,4,64,128]{4,3,2,1,0:T(8,128)S(1)}) custom-call(f32[2]{0:T(128)S(1)} %multiply_add_fusion.inflow_ref, f32[2,4,4,64,128]{4,3,2,1,0:T(8,128)S(1)} %copy-done, f32[2,4,4,64,128]{4,3,2,1,0:T(8,128)S(1)} %copy-done.1, f32[2,14,64,128]{3,2,1,0:T(8,128)} %collective-permute-done.low_ref, ...), custom_call_target="tpu_custom_call" | custom-call | flops 40000000 | bytes 8000000 | tf_op jit(solution)/shard_map/stencil/pallas_call | solution.py:208
  102.3 0.0 copy-start.3
  102.3 1.0 copy-done.3
  103.3 0.0 all-to-all-done.1.t_ref
  103.3 0.0 copy-start.4
  103.3 1.2 %copy-done.4 = f32[2,4,4,64,128]{4,3,2,1,0:T(8,128)S(1)} copy-done((f32[2,4,4,64,128]{4,3,2,1,0:T(8,128)S(1)}, f32[2,4,4,64,128]{4,3,2,1,0:T(8,128)}, u32[]{:S(2)}) %copy-start.4) | copy-done | bytes 1048600
  104.5 2.8 %add_time.1 = (f32[2,4,4,64,128]{4,3,2,1,0:T(8,128)}, f32[2,4,4,64,128]{4,3,2,1,0:T(8,128)}) custom-call(f32[2,4,4,64,128]{4,3,2,1,0:T(8,128)S(1)} %get-tuple-element.4.f_ref, f32[2,4,4,64,128]{4,3,2,1,0:T(8,128)S(1)} %copy-done.4, f32[8,2,6,4,8,128]{5,4,3,2,1,0:T(8,128)} %all-to-all-done.1.t_ref), custom_call_target="tpu_custom_call" | custom-call | tf_op jit(solution)/shard_map/add_time/pallas_call | solution.py:273
  (2 shorter events, 0.1 us)
Async XLA Ops:
  0.6 1.1 %slice-start = ((f32[2,4,4,64,128]{4,3,2,1,0:T(8,128)}), f32[2,3,4,64,128]{4,3,2,1,0:T(8,128)S(1)}, s32[]{:S(2)}) async-start(f32[2,4,4,64,128]{4,3,2,1,0:T(8,128)} %flow_ref.1), calls=%async_computation.2 | async-start | bytes 1572864 | tf_op jit(solution)/shard_map/slice | solution.py:302
  0.6 1.4 %slice-start.1 = ((f32[2,4,4,64,128]{4,3,2,1,0:T(8,128)}), f32[2,3,4,64,128]{4,3,2,1,0:T(8,128)S(1)}, s32[]{:S(2)}) async-start(f32[2,4,4,64,128]{4,3,2,1,0:T(8,128)} %adj_ref.1), calls=%async_computation.3 | async-start | bytes 1572864 | tf_op jit(solution)/shard_map/slice | solution.py:302
  3.4 5.5 %copy-start = (f32[2,4,4,64,128]{4,3,2,1,0:T(8,128)S(1)}, f32[2,4,4,64,128]{4,3,2,1,0:T(8,128)}, u32[]{:S(2)}) copy-start(f32[2,4,4,64,128]{4,3,2,1,0:T(8,128)} %flow_ref.1) | copy-start | bytes 3145732
  3.4 6.3 %copy-start.1 = (f32[2,4,4,64,128]{4,3,2,1,0:T(8,128)S(1)}, f32[2,4,4,64,128]{4,3,2,1,0:T(8,128)}, u32[]{:S(2)}) copy-start(f32[2,4,4,64,128]{4,3,2,1,0:T(8,128)} %adj_ref.1) | copy-start | bytes 3145732
  3.4 28.7 %all-to-all-start = ((f32[8,2,6,4,8,128]{5,4,3,2,1,0:T(8,128)}), f32[8,2,6,4,8,128]{5,4,3,2,1,0:T(8,128)}, u32[]{:S(2)}, u32[]{:S(2)}) async-start(f32[8,2,6,4,8,128]{5,4,3,2,1,0:T(8,128)} %copy_bitcast_fusion), calls=%async_computation | async-start | bytes 3145728 | tf_op jit(solution)/shard_map/all_to_all | solution.py:304
  34.9 1.1 %copy-start.2 = (f32[16,6,4,8,128]{4,3,2,1,0:T(8,128)}, f32[16,6,4,8,128]{4,3,2,1,0:T(8,128)S(1)}, u32[]{:S(2)}) copy-start(f32[16,6,4,8,128]{4,3,2,1,0:T(8,128)S(1)} %time_derivative.1) | copy-start | bytes 4718596
  36.0 67.2 %all-to-all-start.1 = ((f32[8,2,6,4,8,128]{5,4,3,2,1,0:T(8,128)}), f32[8,2,6,4,8,128]{5,4,3,2,1,0:T(8,128)}, u32[]{:S(2)}, u32[]{:S(2)}) async-start(f32[8,2,6,4,8,128]{5,4,3,2,1,0:T(8,128)} %bitcast.25), calls=%async_computation.1 | async-start | bytes 3145728 | tf_op jit(solution)/shard_map/all_to_all | solution.py:307
  41.7 40.5 %copy-start.7 = (f32[4,64,128]{2,1,0:T(8,128)S(1)}, f32[4,64,128]{2,1,0:T(8,128)}, u32[]{:S(2)}) copy-start(f32[4,64,128]{2,1,0:T(8,128)} %density_ref.1) | copy-start | bytes 393220
  41.7 40.5 %copy-start.8 = (s32[4,64,128]{2,1,0:T(8,128)S(1)}, s32[4,64,128]{2,1,0:T(8,128)}, u32[]{:S(2)}) copy-start(s32[4,64,128]{2,1,0:T(8,128)} %mask_ref.1) | copy-start | bytes 393220
  41.8 40.5 %copy-start.9 = (s32[4,64,128]{2,1,0:T(8,128)S(1)}, s32[4,64,128]{2,1,0:T(8,128)}, u32[]{:S(2)}) copy-start(s32[4,64,128]{2,1,0:T(8,128)} %labels_ref.1) | copy-start | bytes 393220
  42.8 38.5 %collective-permute-start.1 = (f32[2,14,64,128]{3,2,1,0:T(8,128)}, f32[2,14,64,128]{3,2,1,0:T(8,128)S(1)}, u32[]{:S(2)}, u32[]{:S(2)}) collective-permute-start(f32[2,14,64,128]{3,2,1,0:T(8,128)} %pad_maximum_fusion.1), channel_id=1, source_target_pairs={{1,0},{2,1},{3,2},{4,3},{5,4},{6,5},{7,6},{8,7},{9,8},{10,9},{11,1... | collective-permute-start | bytes 2752520 | tf_op jit(solution)/shard_map/ppermute | solution.py:300
  47.3 34.9 %collective-permute-start = (f32[2,14,64,128]{3,2,1,0:T(8,128)}, f32[2,14,64,128]{3,2,1,0:T(8,128)}, u32[]{:S(2)}, u32[]{:S(2)}) collective-permute-start(f32[2,14,64,128]{3,2,1,0:T(8,128)} %pad_maximum_fusion), channel_id=1, source_target_pairs={{0,1},{1,2},{2,3},{3,4},{4,5},{5,6},{6,7},{7,8},{8,9},{9,10},{10,1... | collective-permute-start | bytes 2752520 | tf_op jit(solution)/shard_map/ppermute | solution.py:297
  81.3 0.9 copy-start.5
  82.2 1.2 %copy-start.6 = (f32[2,14,64,128]{3,2,1,0:T(8,128)S(1)}, f32[2,14,64,128]{3,2,1,0:T(8,128)}, u32[]{:S(2)}) copy-start(f32[2,14,64,128]{3,2,1,0:T(8,128)} %copy-done.5) | copy-start | bytes 2752516
  102.3 1.0 copy-start.3
  103.3 1.2 %copy-start.4 = (f32[2,4,4,64,128]{4,3,2,1,0:T(8,128)S(1)}, f32[2,4,4,64,128]{4,3,2,1,0:T(8,128)}, u32[]{:S(2)}) copy-start(f32[2,4,4,64,128]{4,3,2,1,0:T(8,128)} %copy-done.3) | copy-start | bytes 3145732
where the time goes:
time: 108 us; the launch traced here: 107 us
  waiting for transfers between devices  50.2 us (46%)
  Pallas kernels  24.5 us (23%)
  starting transfers between devices  18.4 us (17%)
  local copies, waits for them, and re-layouts  8.57 us (8%)
  other arithmetic  4.78 us (4%)
    ppermute x1, waiting for transfers between devices, on_device(): lax.ppermute(boundary(flow, adj, slice(0, 2), 0), 'space', [(i + 1, i) fo...  28.8 us
    all_to_all x1, waiting for transfers between devices, on_device(): gathered = lax.all_to_all(both, 'tm', 0, 0, tiled=True)  21.4 us
    pallas_call x1, Pallas kernels, stencil(): pl.pallas_call(stencil_kernel, out_shape=(shape, shape), in_specs=[pl.Blo...  18.9 us
    all_to_all x1, starting transfers between devices, on_device(): gathered = lax.all_to_all(both, 'tm', 0, 0, tiled=True)  5.51 us
    unnamed x20, local copies, waits for them, and re-layouts  5.45 us
    ppermute x1, starting transfers between devices, on_device(): lax.ppermute(boundary(flow, adj, slice(PLANES - 2, PLANES), PLANES - 1),...  5.1 us
    all_to_all x1, starting transfers between devices, on_device(): time_part = lax.all_to_all(derived, 'tm', 0, 0, tiled=True)  4.3 us
    ppermute x1, starting transfers between devices, on_device(): lax.ppermute(boundary(flow, adj, slice(0, 2), 0), 'space', [(i + 1, i) fo...  3.52 us
  transfers between devices with their start and end apart: 4, of which 2 were waited for; matrix products, arithmetic and copies ran while one was open for 5% of the time, Pallas kernels for 18%

commit v1 on v0

v1 whole, which is shorter than its diff:
```python
import functools

import jax
import jax.numpy as jnp
from jax import lax
from jax.experimental import pallas as pl
from jax.experimental.pallas import tpu as pltpu
from jax.sharding import PartitionSpec as P
import numpy as np

NT = 16
NU_INF = 0.0616
NU_ZERO = 1.0
LAMBDA_SQ = 3.313 * 3.313
POWER = (0.3568 - 1.0) / 2.0
BRINKMAN_MAX = 8.0
RAMP_SHAPE = 0.1
TIME_SCALE = 0.25

PLANES = 4
ROWS = 64
LANES = 128
TOP = 8
PADDED = ROWS + 2 * TOP
TILE = 16
UNROLL = 2
VMEM_LIMIT = 56 << 20
EARLY_COST = 40_000_000_000
LATE_COST = 40_000_000_000
ADD_LIMIT = 12 << 20

MU_A = 0.25 * NU_INF
MU_B = 0.25 * (NU_ZERO - NU_INF)
SHEAR = LAMBDA_SQ / 8.0
DMU = (NU_ZERO - NU_INF) * POWER * LAMBDA_SQ / 16.0


def viscosity(square_sum):
    q = 1.0 + SHEAR * square_sum
    log_q = jnp.log(q)
    return MU_A + MU_B * jnp.exp(POWER * log_q), DMU * jnp.exp((POWER - 1.0) * log_q)


def outer_cell(u, lam, axis):
    strain = [u[j] + u[j] if j == axis else u[j] for j in range(3)]
    rate = [lam[j] + lam[j] if j == axis else lam[j] for j in range(3)]
    others = [j for j in range(3) if j != axis]
    square = sum(strain[j] * strain[j] for j in others)
    cross = sum(strain[j] * rate[j] for j in others)
    square = square + square + strain[axis] * strain[axis]
    cross = cross + cross + strain[axis] * rate[axis]
    mu, dmu = viscosity(square)
    slope = dmu * cross
    return [mu * s for s in strain], [mu * e + slope * s for s, e in zip(strain, rate)]


def stencil_tools(inflow_ref, w, tx, fx, ty, fy, out_f, out_a, density_ref, mask_ref, labels_ref):
    lane = lax.broadcasted_iota(jnp.int32, (TILE, LANES), 1)
    is_first = lane == 0
    is_last = lane == LANES - 1

    def along_z(f):
        up = jnp.where(is_last, 0.0, pltpu.roll(f, LANES - 1, 1))
        down = jnp.where(is_first, 0.0, pltpu.roll(f, 1, 1))
        return up - down

    def along_z_outer(f, outer):
        up = jnp.where(is_last, -outer, pltpu.roll(f, LANES - 1, 1))
        down = jnp.where(is_first, outer, pltpu.roll(f, 1, 1))
        return up - down

    def tile_work(i, p, t, interior):
        r = TOP + pl.multiple_of(t * TILE, 8)
        here = pl.ds(r, TILE)
        u = [w[i, j, p, here, :] for j in range(3)]
        lam = [w[i, 3 + j, p, here, :] for j in range(3)]
        grads, rates = [], []
        for base, values, into in ((0, u, grads), (3, lam, rates)):
            into.append([w[i, base + j, p + 1, here, :] - w[i, base + j, p - 1, here, :] for j in range(3)])
            into.append(
                [w[i, base + j, p, pl.ds(r + 1, TILE), :] - w[i, base + j, p, pl.ds(r - 1, TILE), :] for j in range(3)]
            )
            into.append([along_z(v) for v in values])
        strain = [[grads[k][j] + grads[j][k] for k in range(3)] for j in range(3)]
        rate = [[rates[k][j] + rates[j][k] for k in range(3)] for j in range(3)]
        pairs = ((0, 1), (0, 2), (1, 2))
        square = sum(strain[j][k] * strain[j][k] for j, k in pairs)
        cross = sum(strain[j][k] * rate[j][k] for j, k in pairs)
        square = square + square + sum(strain[j][j] * strain[j][j] for j in range(3))
        cross = cross + cross + sum(strain[j][j] * rate[j][j] for j in range(3))
        mu, dmu = viscosity(square)
        slope = dmu * cross
        half_u = [0.5 * v for v in u]
        half_p = 0.5 * w[i, 6, p, here, :]
        half_q = 0.5 * w[i, 7, p, here, :]

        def flux(j, k):
            t_jk = mu * strain[j][k]
            f_jk = mu * rate[j][k] + slope * strain[j][k] + half_u[k] * lam[j]
            if j == k:
                t_jk, f_jk = t_jk - half_p, f_jk + half_q
            return t_jk, f_jk

        for j in range(3):
            t_jk, f_jk = flux(j, 0)
            tx[i, j, p, pl.ds(r - TOP, TILE), :] = t_jk
            fx[i, j, p, pl.ds(r - TOP, TILE), :] = f_jk
        if not interior:
            return
        q = p - 2
        out_rows = pl.ds(r - TOP, TILE)
        for j in range(3):
            t_jk, f_jk = flux(j, 1)
            ty[j, q, here, :] = t_jk
            fy[j, q, here, :] = f_jk
        outer_t, outer_f = outer_cell(u, lam, 2)
        design = jnp.where(mask_ref[q, out_rows, :] == 1, density_ref[q, out_rows, :], 1.0)
        label = labels_ref[q, out_rows, :]
        ramp = (BRINKMAN_MAX * RAMP_SHAPE) * (1.0 - design) / (RAMP_SHAPE + design)
        penalty = jnp.where(label == 0, ramp, BRINKMAN_MAX)
        target = jnp.where(label == 2, inflow_ref[i], 0.0)
        half_lam = [0.5 * v for v in lam]
        for j in range(3):
            t_jk, f_jk = flux(j, 2)
            shifted = u[j] - target if j == 0 else u[j]
            out_f[i, j, q, out_rows, :] = (
                sum(half_u[k] * grads[k][j] for k in range(3)) - along_z_outer(t_jk, outer_t[j]) + penalty * shifted
            )
            out_a[i, j, q, out_rows, :] = (
                sum(half_lam[k] * grads[j][k] for k in range(3)) - along_z_outer(f_jk, outer_f[j]) + penalty * lam[j]
            )
        out_f[i, 3, q, out_rows, :] = 0.25 * (strain[0][0] + strain[1][1] + strain[2][2])
        out_a[i, 3, q, out_rows, :] = -0.25 * (rate[0][0] + rate[1][1] + rate[2][2])

    def y_edges(i, q):
        p = q + 2
        for first, keep, row, sign in ((TOP, 0, TOP - 1, 1.0), (TOP + ROWS - 8, 7, TOP + ROWS, -1.0)):
            u = [w[i, j, p, first : first + 8, :] for j in range(3)]
            lam = [w[i, 3 + j, p, first : first + 8, :] for j in range(3)]
            outer_t, outer_f = outer_cell(u, lam, 1)
            for j in range(3):
                ty[j, q, row : row + 1, :] = sign * outer_t[j][keep : keep + 1]
                fy[j, q, row : row + 1, :] = sign * outer_f[j][keep : keep + 1]

    def collect(i, p, t, with_x, with_y):
        q = p - 2
        r = pl.multiple_of(t * TILE, 8)
        for out, x_flux, y_flux in ((out_f, tx, ty), (out_a, fx, fy)):
            for j in range(3):
                total = out[i, j, q, pl.ds(r, TILE), :]
                if with_x:
                    total -= x_flux[i, j, p + 1, pl.ds(r, TILE), :] - x_flux[i, j, p - 1, pl.ds(r, TILE), :]
                if with_y:
                    total -= (
                        y_flux[j, q, pl.ds(r + TOP + 1, TILE), :] - y_flux[j, q, pl.ds(r + TOP - 1, TILE), :]
                    )
                out[i, j, q, pl.ds(r, TILE), :] = total

    def over(first, planes, work):
        tiles = ROWS // TILE

        def step(n, _):
            work(first + n // tiles, n % tiles)
            return 0

        lax.fori_loop(0, planes * tiles, step, 0, unroll=UNROLL)

    return tile_work, y_edges, collect, over


def clear_edges(w, i, first, planes):
    zero = jnp.zeros((TOP, LANES), jnp.float32)

    def clear(p, _):
        for c in range(6):
            w[i, c, first + p, 0:TOP, :] = zero
            w[i, c, first + p, TOP + ROWS : PADDED, :] = zero
        return 0

    lax.fori_loop(0, planes, clear, 0)


def early_kernel(
    core_ref, inflow_ref, flow_ref, adj_ref, halo_ref, density_hbm, mask_hbm, labels_hbm,
    flow_out, adj_out, tx_out, fx_out,
    out_f, out_a, density_ref, mask_ref, labels_ref, w, tx, fx, ty, fy, sems, cell_sems, out_sems,
):
    insts = out_f.shape[0]
    core = core_ref[0]
    data = pl.ds(TOP, ROWS)
    reads, writes = [], []
    three = pl.ds(1 - core, 3)
    for i in range(insts):
        copies = []
        for source, base, last in ((flow_ref, 0, 6), (adj_ref, 3, 7)):
            copies.append((source.at[i, 0:3], w.at[i, base : base + 3, 2:6, data, :]))
            copies.append((source.at[i, 3], w.at[i, last, 2:6, data, :]))
        for c in range(6):
            copies.append((halo_ref.at[i, 2 * c : 2 * c + 2], w.at[i, c, pl.ds(6 - 6 * core, 2), data, :]))
        copies.append((halo_ref.at[i, 12:14], w.at[i, 6:8, 6 - 5 * core, data, :]))
        reads.append([pltpu.make_async_copy(a, b, sems.at[i, k]) for k, (a, b) in enumerate(copies)])
        copies = [(a.at[i, :, three], b.at[i, :, three]) for a, b in ((out_f, flow_out), (out_a, adj_out))]
        copies += [(a.at[i, :, 3:5], b.at[i]) for a, b in ((tx, tx_out), (fx, fx_out))]
        writes.append([pltpu.make_async_copy(a, b, out_sems.at[i, k]) for k, (a, b) in enumerate(copies)])
    cells = ((density_hbm, density_ref), (mask_hbm, mask_ref), (labels_hbm, labels_ref))
    reads[0] += [pltpu.make_async_copy(a, b, cell_sems.at[k]) for k, (a, b) in enumerate(cells)]
    for group in reads:
        for h in group:
            h.start()
    for i in range(insts):
        clear_edges(w, i, 0, 8)
    tile_work, y_edges, collect, over = stencil_tools(
        inflow_ref, w, tx, fx, ty, fy, out_f, out_a, density_ref, mask_ref, labels_ref
    )
    for i in range(insts):
        for h in reads[i]:
            h.wait()
        over(6 - 5 * core, 1, lambda p, t: tile_work(i, p, t, False))
        over(3 - core, 3, lambda p, t: tile_work(i, p, t, True))

        def edges(n, _):
            y_edges(i, 1 - core + n)
            return 0

        lax.fori_loop(0, 3, edges, 0)
        over(4 - 2 * core, 2, lambda p, t: collect(i, p, t, True, True))
        over(3 + core, 1, lambda p, t: collect(i, p, t, False, True))
        for h in writes[i]:
            h.start()
    for group in writes:
        for h in group:
            h.wait()


def late_kernel(
    core_ref, inflow_ref, flow_ref, adj_ref, far_ref, last_ref, density_hbm, mask_hbm, labels_hbm,
    flow_part, adj_part, tx_part, fx_part, flow_out, adj_out,
    out_f, out_a, density_ref, mask_ref, labels_ref, w, tx, fx, ty, fy, sems, part_sems, cell_sems, out_sems,
):
    insts = out_f.shape[0]
    core = core_ref[0]
    data = pl.ds(TOP, ROWS)
    reads, parts, writes = [], [], []
    pair, partial = pl.ds(2 * core, 2), pl.ds(1 + core, 1)
    for i in range(insts):
        copies = []
        for source, base, last in ((flow_ref, 0, 6), (adj_ref, 3, 7)):
            copies.append((source.at[i, 0:3, pair], w.at[i, base : base + 3, pl.ds(2 + 2 * core, 2), data, :]))
            copies.append((source.at[i, 3, pair], w.at[i, last, pl.ds(2 + 2 * core, 2), data, :]))
        cut = far_ref.shape[0]
        halo_ref = far_ref.at[i] if i < cut else last_ref.at[i - cut]
        for c in range(6):
            copies.append((halo_ref.at[2 * c : 2 * c + 2], w.at[i, c, pl.ds(6 * core, 2), data, :]))
        copies.append((halo_ref.at[12:14], w.at[i, 6:8, 1 + 5 * core, data, :]))
        reads.append([pltpu.make_async_copy(a, b, sems.at[i, k]) for k, (a, b) in enumerate(copies)])
        copies = [(a.at[i, :, partial], b.at[i, :, partial]) for a, b in ((flow_out, out_f), (adj_out, out_a))]
        copies += [(a.at[i], b.at[i, :, 3:5]) for a, b in ((tx_part, tx), (fx_part, fx))]
        parts.append([pltpu.make_async_copy(a, b, part_sems.at[i, k]) for k, (a, b) in enumerate(copies)])
        copies = ((out_f, flow_out), (out_a, adj_out))
        writes.append([pltpu.make_async_copy(a.at[i, :, pair], b.at[i, :, pair], out_sems.at[i, k]) for k, (a, b) in enumerate(copies)])
    cells = ((density_hbm, density_ref), (mask_hbm, mask_ref), (labels_hbm, labels_ref))
    reads[0] += [
        pltpu.make_async_copy(a.at[pl.ds(3 * core, 1)], b.at[pl.ds(3 * core, 1)], cell_sems.at[k])
        for k, (a, b) in enumerate(cells)
    ]
    for i in range(insts):
        for h in reads[i] + parts[i]:
            h.start()
    for i in range(insts):
        clear_edges(w, i, 4 * core, 4)
    tile_work, y_edges, collect, over = stencil_tools(
        inflow_ref, w, tx, fx, ty, fy, out_f, out_a, density_ref, mask_ref, labels_ref
    )
    for i in range(insts):
        for h in reads[i]:
            h.wait()
        over(1 + 5 * core, 1, lambda p, t: tile_work(i, p, t, False))
        over(2 + 3 * core, 1, lambda p, t: tile_work(i, p, t, True))
        y_edges(i, 3 * core)
        for h in parts[i]:
            h.wait()
        over(2 + 3 * core, 1, lambda p, t: collect(i, p, t, True, True))
        over(3 + core, 1, lambda p, t: collect(i, p, t, True, False))
        for h in writes[i]:
            h.start()
    for group in writes:
        for h in group:
            h.wait()


def add_kernel(f_ref, a_ref, times, out_f, out_a, total, sems):
    insts = out_f.shape[0]
    work = [(i, n) for i in range(insts) for n in range(2)]
    reads, writes = [], []
    for k, (i, n) in enumerate(work):
        out = (out_f, out_a)[n].at[i, 0:3]
        reads.append(pltpu.make_async_copy(out, total.at[i, n], sems.at[0, k]))
        writes.append(pltpu.make_async_copy(total.at[i, n], out, sems.at[1, k]))
    for read in reads:
        read.start()
    for (i, n), read, write in zip(work, reads, writes):
        read.wait()
        for j in range(3):
            for b in range(2 * PLANES):
                q, rows = block_cells(b)
                total[i, n, j, q, rows, :] = total[i, n, j, q, rows, :] + times[b, i, 3 * n + j]
        write.start()
    for write in writes:
        write.wait()


def add_time(flow_part, adj_part, time_part):
    space = pl.BlockSpec(memory_space=pltpu.HBM)
    insts = flow_part.shape[0]
    shape = jax.ShapeDtypeStruct(flow_part.shape, jnp.float32)
    return pl.pallas_call(
        add_kernel,
        out_shape=(shape, shape),
        in_specs=[space] * 2 + [pl.BlockSpec(memory_space=pltpu.VMEM)],
        out_specs=[space] * 2,
        scratch_shapes=[
            pltpu.VMEM((insts, 2, 3) + flow_part.shape[2:], jnp.float32),
            pltpu.SemaphoreType.DMA((2, 2 * insts)),
        ],
        compiler_params=pltpu.CompilerParams(vmem_limit_bytes=ADD_LIMIT),
        input_output_aliases={0: 0, 1: 1},
        name="add_time",
    )(flow_part, adj_part, time_part)


def stencil(kernel, name, cost, out_shapes, core, inflow, flow, adj, halos, cells, *parts):
    insts = flow.shape[0]
    space = pl.BlockSpec(memory_space=pltpu.HBM)
    scalar = pl.BlockSpec(memory_space=pltpu.SMEM)
    like = lambda a: pltpu.VMEM(a.shape, a.dtype)
    late = len(parts) > 0
    return pl.pallas_call(
        kernel,
        out_shape=[jax.ShapeDtypeStruct(s, jnp.float32) for s in out_shapes],
        in_specs=[scalar] * 2 + [space] * (2 + len(halos) + len(cells) + len(parts)),
        out_specs=[space] * len(out_shapes),
        scratch_shapes=[like(flow), like(flow)]
        + [like(a) for a in cells]
        + [pltpu.VMEM((insts, 8, 8, PADDED, LANES), jnp.float32)]
        + [pltpu.VMEM((insts, 3, 8, ROWS, LANES), jnp.float32)] * 2
        + [pltpu.VMEM((3, PLANES, PADDED, LANES), jnp.float32)] * 2
        + [pltpu.SemaphoreType.DMA((insts, 11))]
        + ([pltpu.SemaphoreType.DMA((insts, 4))] if late else [])
        + [pltpu.SemaphoreType.DMA((3,)), pltpu.SemaphoreType.DMA((insts, 4))],
        compiler_params=pltpu.CompilerParams(vmem_limit_bytes=VMEM_LIMIT),
        cost_estimate=pl.CostEstimate(flops=cost, bytes_accessed=8_000_000, transcendentals=400_000),
        input_output_aliases={5 + len(halos) + len(cells) - 1 + k: k for k in range(2)} if late else {},
        name=name,
    )(core, inflow, flow, adj, *halos, *cells, *parts)


def spectral_row():
    k = np.arange(1, 8)
    return [float(v) for v in TIME_SCALE * 0.5 * np.where(k % 2 == 0, 1.0, -1.0) / np.tan(np.pi * k / NT)]


def time_kernel(x_ref, sent_hbm, out_hbm, out_ref, sems):
    comps, tiles = x_ref.shape[1], x_ref.shape[2] // 8
    writes = [pltpu.make_async_copy(out_ref.at[:, c], out_hbm.at[:, c], sems.at[c]) for c in range(comps)]
    for c in range(comps):
        coef = [v if c < comps // 2 else -v for v in spectral_row()]

        def step(n, _):
            rows = pl.ds(pl.multiple_of(n * 8, 8), 8)
            x = [x_ref[m, c, rows, :] for m in range(NT)]
            for m in range(NT // 2):
                diff = [x[(m - k) % NT] - x[(m + k) % NT] for k in range(1, 8)]
                out_ref[m, c, rows, :] = sum(coef[k - 1] * diff[k - 1] for k in range(1, 8))
                out_ref[m + 8, c, rows, :] = -sum(coef[k - 1] * diff[7 - k] for k in range(1, 8))
            return 0

        lax.fori_loop(0, tiles, step, 0, unroll=2)
        writes[c].start()
    for h in writes:
        h.wait()


def time_derivative(x, sent):
    return pl.pallas_call(
        time_kernel,
        out_shape=jax.ShapeDtypeStruct(x.shape, jnp.float32),
        in_specs=[pl.BlockSpec(memory_space=pltpu.VMEM), pl.BlockSpec(memory_space=pltpu.HBM)],
        out_specs=pl.BlockSpec(memory_space=pltpu.HBM),
        scratch_shapes=[pltpu.VMEM(x.shape, jnp.float32), pltpu.SemaphoreType.DMA((x.shape[1],))],
        compiler_params=pltpu.CompilerParams(vmem_limit_bytes=8 << 20),
        cost_estimate=pl.CostEstimate(flops=12_000_000, bytes_accessed=3_200_000, transcendentals=0),
        input_output_aliases={1: 0},
        name="time_derivative",
    )(x, sent)


def block_cells(b):
    half = ROWS // 2
    return b // 2, slice(b % 2 * half, (b % 2 + 1) * half)


def halo_copies(flow_ref, adj_ref, ref, insts, first, near):
    copies = []
    for j in range(3):
        copies.append((flow_ref.at[insts, j, pl.ds(first, 2)], ref.at[:, 2 * j : 2 * j + 2]))
        copies.append((adj_ref.at[insts, j, pl.ds(first, 2)], ref.at[:, 6 + 2 * j : 8 + 2 * j]))
    copies.append((flow_ref.at[insts, 3, pl.ds(near, 1)], ref.at[:, 12:13]))
    copies.append((adj_ref.at[insts, 3, pl.ds(near, 1)], ref.at[:, 13:14]))
    return copies


def block_copies(flow_ref, adj_ref, ref, b):
    q, rows = block_cells(b)
    return [(flow_ref.at[:, 0:3, q, rows], ref.at[b, :, 0:3]), (adj_ref.at[:, 0:3, q, rows], ref.at[b, :, 3:6])]


def through_vmem(groups, sems):
    flat = [c for copies, _ in groups for c in copies] + [write for _, write in groups]
    handles = [pltpu.make_async_copy(a, b, sems.at[i]) for i, (a, b) in enumerate(flat)]
    writes = handles[len(handles) - len(groups) :]
    for h in handles[: len(handles) - len(groups)]:
        h.start()
    done = 0
    for (copies, _), write in zip(groups, writes):
        for h in handles[done : done + len(copies)]:
            h.wait()
        done += len(copies)
        write.start()
    for write in writes:
        write.wait()


def pack_halo_kernel(core_ref, flow_ref, adj_ref, far_ref, last_ref, near_ref, far, last, near, sems):
    core = core_ref[0]
    insts = flow_ref.shape[0]
    cut = far.shape[0]
    groups = [(halo_copies(flow_ref, adj_ref, near, slice(0, insts), 2 - 2 * core, 3 - 3 * core), (near, near_ref))]
    for ref, out, which in ((far, far_ref, slice(0, cut)), (last, last_ref, slice(cut, insts))):
        groups.append((halo_copies(flow_ref, adj_ref, ref, which, 2 * core, 3 * core), (ref, out)))
    through_vmem(groups, sems)


def pack_block_kernel(core_ref, flow_ref, adj_ref, blocks_ref, blocks, sems):
    groups = [
        (block_copies(flow_ref, adj_ref, blocks, b), (blocks.at[b], blocks_ref.at[b])) for b in range(2 * PLANES)
    ]
    through_vmem(groups, sems)


def pack(kernel, name, core, flow, adj, shapes):
    space = pl.BlockSpec(memory_space=pltpu.HBM)
    return pl.pallas_call(
        kernel,
        out_shape=[jax.ShapeDtypeStruct(s, jnp.float32) for s in shapes],
        in_specs=[pl.BlockSpec(memory_space=pltpu.SMEM)] + [space] * 2,
        out_specs=[space] * len(shapes),
        scratch_shapes=[pltpu.VMEM(s, jnp.float32) for s in shapes] + [pltpu.SemaphoreType.DMA((7 * PLANES,))],
        compiler_params=pltpu.CompilerParams(vmem_limit_bytes=VMEM_LIMIT),
        name=name,
    )(core, flow, adj)


def on_device(flow, adj, density, mask, labels):
    insts = flow.shape[0]
    count = lax.axis_size("space")
    instances = lax.axis_index("tm") * insts + jnp.arange(insts, dtype=jnp.int32)
    inflow = 1.0 + 0.5 * jnp.sin(2.0 * jnp.pi * instances.astype(jnp.float32) / NT)

    core = lax.axis_index("space") % 2
    core = core.reshape(1)
    halo = (insts, 14, ROWS, LANES)
    cut = insts // 2
    halves = [(cut,) + halo[1:], (insts - cut,) + halo[1:]]
    far, last, near = pack(pack_halo_kernel, "pack_halo", core, flow, adj, halves + [halo])
    across = [p for i in range(1, count - 1, 2) for p in ((i, i + 1), (i + 1, i))]
    far, last = lax.ppermute(far, "space", across), lax.ppermute(last, "space", across)
    near = lax.ppermute(near, "space", [p for i in range(0, count, 2) for p in ((i, i + 1), (i + 1, i))])
    (blocks,) = pack(pack_block_kernel, "pack_block", core, flow, adj, [(2 * PLANES, insts, 6, ROWS // 2, LANES)])
    gathered = lax.all_to_all(blocks, "tm", 0, 0, tiled=True)
    cells = (density, mask, labels)
    edge = (insts, 3, 2, ROWS, LANES)
    parts = stencil(
        early_kernel, "early", EARLY_COST, [flow.shape] * 2 + [edge] * 2, core, inflow, flow, adj, [near], cells
    )
    gathered, *parts = lax.optimization_barrier((gathered, *parts))
    by_time = (NT,) + blocks.shape[2:]
    derived = time_derivative(gathered.reshape(by_time), blocks.reshape(by_time))
    time_part = lax.all_to_all(derived.reshape(blocks.shape), "tm", 0, 0, tiled=True)
    late = stencil(late_kernel, "late", LATE_COST, [flow.shape] * 2, core, inflow, flow, adj, [far, last], cells, *parts)
    return add_time(*late, time_part)


def solution(mesh):
    split = P("tm", None, "space", None, None)
    cells = P("space", None, None)
    return jax.shard_map(
        on_device,
        mesh=mesh,
        in_specs=(split, split, cells, cells, cells),
        out_specs=(split, split),
        check_vma=False,
    )
```

time: 108 us -> 74.9 us (0.69)
  the two profiles are of different devices: /device:TPU:17 before, /device:TPU:13 now
where the time goes in v1:
time: 74.9 us; the launch traced here: 74.5 us
  waiting for transfers between devices  32 us (43%)
  Pallas kernels  21.9 us (29%)
  starting transfers between devices  18.3 us (24%)
  local copies, waits for them, and re-layouts  0.93 us (1%)
    ppermute x1, waiting for transfers between devices, on_device(): lax.ppermute(last, 'space', across)  18.7 us
    pallas_call x2, Pallas kernels, stencil(): pl.pallas_call(kernel, out_shape=[jax.ShapeDtypeStruct(s, jnp.float32) fo...  12.8 us
    all_to_all x1, waiting for transfers between devices, on_device(): gathered = lax.all_to_all(blocks, 'tm', 0, 0, tiled=True)  12.4 us
    all_to_all x1, starting transfers between devices, on_device(): gathered = lax.all_to_all(blocks, 'tm', 0, 0, tiled=True)  5.74 us
    ppermute x1, starting transfers between devices, on_device(): lax.ppermute(far, 'space', across)  5.68 us
    pallas_call x2, Pallas kernels, pack(): pl.pallas_call(kernel, out_shape=[jax.ShapeDtypeStruct(s, jnp.float32) fo...  5.11 us
    all_to_all x1, starting transfers between devices, on_device(): lax.all_to_all(derived.reshape(blocks.shape), 'tm', 0, 0, tiled=True)  4.26 us
    pallas_call x1, Pallas kernels, add_time(): pl.pallas_call(add_kernel, out_shape=(shape, shape), in_specs=[space] * 2...  2.24 us
  transfers between devices with their start and end apart: 5, of which 3 were waited for; matrix products, arithmetic and copies ran while one was open for 1% of the time, Pallas kernels for 23%

profile of v1, /device:TPU:13, one launch (start us, length us, event | category | flops | bytes accessed | tf_op | source)
XLA Modules:
  0.0 74.5 jit_solution(4851184488080019780)
XLA Ops:
  0.6 2.7 %pack_halo.1 = (f32[1,14,64,128]{3,2,1,0:T(8,128)}, f32[1,14,64,128]{3,2,1,0:T(8,128)}, f32[2,14,64,128]{3,2,1,0:T(8,128)}) custom-call(s32[1]{0:T(128)} %bitcast.core_ref, f32[2,4,4,64,128]{4,3,2,1,0:T(8,128)} %flow_ref.7, f32[2,4,4,64,128]{4,3,2,1,0:T(8,128)} %adj_ref.7), custom_call_target="tpu_custom_call" | custom-call | tf_op jit(solution)/shard_map/pack_halo/pallas_call | solution.py:452
  3.3 0.8 %collective-permute-start.2 = (f32[2,14,64,128]{3,2,1,0:T(8,128)}, f32[2,14,64,128]{3,2,1,0:T(8,128)S(1)}, u32[]{:S(2)}, u32[]{:S(2)}) collective-permute-start(f32[2,14,64,128]{3,2,1,0:T(8,128)} %get-tuple-element.18), channel_id=1, source_target_pairs={{0,1},{1,0},{2,3},{3,2},{4,5},{5,4},{6,7},{7,6},{8,9},{9,8},{10,11... | collective-permute-start | bytes 2752520 | tf_op jit(solution)/shard_map/ppermute | solution.py:477
  4.1 2.4 %pack_block.1 = f32[8,2,6,32,128]{4,3,2,1,0:T(8,128)} custom-call(s32[1]{0:T(128)} %bitcast.core_ref, f32[2,4,4,64,128]{4,3,2,1,0:T(8,128)} %flow_ref.7, f32[2,4,4,64,128]{4,3,2,1,0:T(8,128)} %adj_ref.7), custom_call_target="tpu_custom_call" | custom-call | tf_op jit(solution)/shard_map/pack_block/pallas_call | solution.py:452
  6.5 0.0 copy-start.2
  6.5 0.0 copy-start.1
  6.5 5.7 %all-to-all-start = ((f32[8,2,6,32,128]{4,3,2,1,0:T(8,128)}), f32[8,2,6,32,128]{4,3,2,1,0:T(8,128)S(1)}, u32[]{:S(2)}, u32[]{:S(2)}) async-start(f32[8,2,6,32,128]{4,3,2,1,0:T(8,128)} %pack_block.1), calls=%async_computation | async-start | bytes 3145728 | tf_op jit(solution)/shard_map/all_to_all | solution.py:479
  12.3 0.0 copy-done.2
  12.3 5.7 %collective-permute-start = (f32[1,14,64,128]{3,2,1,0:T(8,128)S(1)}, f32[1,14,64,128]{3,2,1,0:T(8,128)}, u32[]{:S(2)}, u32[]{:S(2)}) collective-permute-start(f32[1,14,64,128]{3,2,1,0:T(8,128)S(1)} %copy-done.2), channel_id=1, source_target_pairs={{1,2},{2,1},{3,4},{4,3},{5,6},{6,5},{7,8},{8,7},{9,10},{10,9},{11,... | collective-permute-start | bytes 1376264 | tf_op jit(solution)/shard_map/ppermute | solution.py:476
  18.0 0.0 copy-done.1
  18.0 1.9 %collective-permute-start.1 = (f32[1,14,64,128]{3,2,1,0:T(8,128)S(1)}, f32[1,14,64,128]{3,2,1,0:T(8,128)}, u32[]{:S(2)}, u32[]{:S(2)}) collective-permute-start(f32[1,14,64,128]{3,2,1,0:T(8,128)S(1)} %copy-done.1), channel_id=1, source_target_pairs={{1,2},{2,1},{3,4},{4,3},{5,6},{6,5},{7,8},{8,7},{9,10},{10,9},{11,... | collective-permute-start | bytes 1376264 | tf_op jit(solution)/shard_map/ppermute | solution.py:476
  19.9 0.6 multiply_add_fusion.inflow_ref
  20.5 0.0 collective-permute-done.2.halo_ref
  20.5 0.0 copy-start
  20.5 0.9 %copy-done = f32[2,14,64,128]{3,2,1,0:T(8,128)} copy-done((f32[2,14,64,128]{3,2,1,0:T(8,128)}, f32[2,14,64,128]{3,2,1,0:T(8,128)S(1)}, u32[]{:S(2)}) %copy-start) | copy-done | bytes 917528
  21.5 7.7 %early.1 = (f32[2,4,4,64,128]{4,3,2,1,0:T(8,128)}, f32[2,4,4,64,128]{4,3,2,1,0:T(8,128)}, f32[2,3,2,64,128]{4,3,2,1,0:T(8,128)}, f32[2,3,2,64,128]{4,3,2,1,0:T(8,128)}) custom-call(s32[1]{0:T(128)} %bitcast.core_ref, f32[2]{0:T(128)} %multiply_add_fusion.inflow_ref, f32[2,4,4,64,128]{4,3,2,1,0:T(8,128)} %flow_ref.7, f32[2,4,4,64,128]{4,3,2,1,0:T(8,128)} %adj_ref.7, ...), custom_call_target="tpu_custom_call" | custom-call | flops 40000000000 | bytes 8000000 | tf_op jit(solution)/shard_map/early/pallas_call | solution.py:337
  29.1 12.4 %all-to-all-done = f32[8,2,6,32,128]{4,3,2,1,0:T(8,128)S(1)} async-done(((f32[8,2,6,32,128]{4,3,2,1,0:T(8,128)}), f32[8,2,6,32,128]{4,3,2,1,0:T(8,128)S(1)}, u32[]{:S(2)}, u32[]{:S(2)}) %all-to-all-start) | async-done | bytes 1572896 | tf_op jit(solution)/shard_map/all_to_all | solution.py:479
  41.5 1.7 %time_derivative.1 = f32[16,6,32,128]{3,2,1,0:T(8,128)} custom-call(f32[16,6,32,128]{3,2,1,0:T(8,128)S(1)} %bitcast.4, f32[16,6,32,128]{3,2,1,0:T(8,128)} %bitcast.2.sent_hbm), custom_call_target="tpu_custom_call", output_to_operand_aliasing={{}: (1, {})} | custom-call | flops 12000000 | bytes 3200000 | tf_op jit(solution)/shard_map/time_derivative/pallas_call | solution.py:384
  43.3 4.3 %all-to-all-start.1 = ((f32[8,2,6,32,128]{4,3,2,1,0:T(8,128)}), f32[8,2,6,32,128]{4,3,2,1,0:T(8,128)S(1)}, u32[]{:S(2)}, u32[]{:S(2)}) async-start(f32[8,2,6,32,128]{4,3,2,1,0:T(8,128)} %bitcast.3), calls=%async_computation.1 | async-start | bytes 3145728 | tf_op jit(solution)/shard_map/all_to_all | solution.py:488
  47.5 0.9 %collective-permute-done.far_ref = f32[1,14,64,128]{3,2,1,0:T(8,128)} collective-permute-done((f32[1,14,64,128]{3,2,1,0:T(8,128)S(1)}, f32[1,14,64,128]{3,2,1,0:T(8,128)}, u32[]{:S(2)}, u32[]{:S(2)}) %collective-permute-start) | collective-permute-done | bytes 458784 | tf_op jit(solution)/shard_map/ppermute | solution.py:476
  48.4 18.7 %collective-permute-done.1.last_ref = f32[1,14,64,128]{3,2,1,0:T(8,128)} collective-permute-done((f32[1,14,64,128]{3,2,1,0:T(8,128)S(1)}, f32[1,14,64,128]{3,2,1,0:T(8,128)}, u32[]{:S(2)}, u32[]{:S(2)}) %collective-permute-start.1) | collective-permute-done | bytes 458784 | tf_op jit(solution)/shard_map/ppermute | solution.py:476
  67.1 5.1 %late.1 = (f32[2,4,4,64,128]{4,3,2,1,0:T(8,128)}, f32[2,4,4,64,128]{4,3,2,1,0:T(8,128)}) custom-call(s32[1]{0:T(128)} %bitcast.core_ref, f32[2]{0:T(128)} %multiply_add_fusion.inflow_ref, f32[2,4,4,64,128]{4,3,2,1,0:T(8,128)} %flow_ref.7, f32[2,4,4,64,128]{4,3,2,1,0:T(8,128)} %adj_ref.7, ...), custom_call_target="tpu_custom_call", output_to_operand_aliasing={{0}: (9, {}), {1}: (10, {})} | custom-call | flops 40000000000 | bytes 8000000 | tf_op jit(solution)/shard_map/late/pallas_call | solution.py:337
  72.3 0.0 all-to-all-done.1.times
  72.3 2.2 %add_time.1 = (f32[2,4,4,64,128]{4,3,2,1,0:T(8,128)}, f32[2,4,4,64,128]{4,3,2,1,0:T(8,128)}) custom-call(f32[2,4,4,64,128]{4,3,2,1,0:T(8,128)} %get-tuple-element.27.f_ref, f32[2,4,4,64,128]{4,3,2,1,0:T(8,128)} %get-tuple-element.28.a_ref, f32[8,2,6,32,128]{4,3,2,1,0:T(8,128)S(1)} %all-to-all-done.1.times), custom_call_target="tpu_custom_call", output_to_operand_aliasing={{0}: (0, {}), {1}: (1, {})} | custom-call | tf_op jit(solution)/shard_map/add_time/pallas_call | solution.py:316
Async XLA Ops:
  3.3 17.2 %collective-permute-start.2 = (f32[2,14,64,128]{3,2,1,0:T(8,128)}, f32[2,14,64,128]{3,2,1,0:T(8,128)S(1)}, u32[]{:S(2)}, u32[]{:S(2)}) collective-permute-start(f32[2,14,64,128]{3,2,1,0:T(8,128)} %get-tuple-element.18), channel_id=1, source_target_pairs={{0,1},{1,0},{2,3},{3,2},{4,5},{5,4},{6,7},{7,6},{8,9},{9,8},{10,11... | collective-permute-start | bytes 2752520 | tf_op jit(solution)/shard_map/ppermute | solution.py:477
  6.5 5.8 %copy-start.2 = (f32[1,14,64,128]{3,2,1,0:T(8,128)S(1)}, f32[1,14,64,128]{3,2,1,0:T(8,128)}, u32[]{:S(2)}) copy-start(f32[1,14,64,128]{3,2,1,0:T(8,128)} %get-tuple-element.16) | copy-start | bytes 1376260
  6.5 11.4 %copy-start.1 = (f32[1,14,64,128]{3,2,1,0:T(8,128)S(1)}, f32[1,14,64,128]{3,2,1,0:T(8,128)}, u32[]{:S(2)}) copy-start(f32[1,14,64,128]{3,2,1,0:T(8,128)} %get-tuple-element.17) | copy-start | bytes 1376260
  6.5 35.0 %all-to-all-start = ((f32[8,2,6,32,128]{4,3,2,1,0:T(8,128)}), f32[8,2,6,32,128]{4,3,2,1,0:T(8,128)S(1)}, u32[]{:S(2)}, u32[]{:S(2)}) async-start(f32[8,2,6,32,128]{4,3,2,1,0:T(8,128)} %pack_block.1), calls=%async_computation | async-start | bytes 3145728 | tf_op jit(solution)/shard_map/all_to_all | solution.py:479
  12.3 36.2 %collective-permute-start = (f32[1,14,64,128]{3,2,1,0:T(8,128)S(1)}, f32[1,14,64,128]{3,2,1,0:T(8,128)}, u32[]{:S(2)}, u32[]{:S(2)}) collective-permute-start(f32[1,14,64,128]{3,2,1,0:T(8,128)S(1)} %copy-done.2), channel_id=1, source_target_pairs={{1,2},{2,1},{3,4},{4,3},{5,6},{6,5},{7,8},{8,7},{9,10},{10,9},{11,... | collective-permute-start | bytes 1376264 | tf_op jit(solution)/shard_map/ppermute | solution.py:476
  18.0 49.1 %collective-permute-start.1 = (f32[1,14,64,128]{3,2,1,0:T(8,128)S(1)}, f32[1,14,64,128]{3,2,1,0:T(8,128)}, u32[]{:S(2)}, u32[]{:S(2)}) collective-permute-start(f32[1,14,64,128]{3,2,1,0:T(8,128)S(1)} %copy-done.1), channel_id=1, source_target_pairs={{1,2},{2,1},{3,4},{4,3},{5,6},{6,5},{7,8},{8,7},{9,10},{10,9},{11,... | collective-permute-start | bytes 1376264 | tf_op jit(solution)/shard_map/ppermute | solution.py:476
  20.5 0.9 %copy-start = (f32[2,14,64,128]{3,2,1,0:T(8,128)}, f32[2,14,64,128]{3,2,1,0:T(8,128)S(1)}, u32[]{:S(2)}) copy-start(f32[2,14,64,128]{3,2,1,0:T(8,128)S(1)} %collective-permute-done.2.halo_ref) | copy-start | bytes 2752516
  43.3 29.0 %all-to-all-start.1 = ((f32[8,2,6,32,128]{4,3,2,1,0:T(8,128)}), f32[8,2,6,32,128]{4,3,2,1,0:T(8,128)S(1)}, u32[]{:S(2)}, u32[]{:S(2)}) async-start(f32[8,2,6,32,128]{4,3,2,1,0:T(8,128)} %bitcast.3), calls=%async_computation.1 | async-start | bytes 3145728 | tf_op jit(solution)/shard_map/all_to_all | solution.py:488

commit v2 on v1

--- a/solution.py
+++ b/solution.py
@@ -25,9 +25,10 @@
 TILE = 16
 UNROLL = 2
 VMEM_LIMIT = 56 << 20
-EARLY_COST = 40_000_000_000
+EARLY_COST = 20_000_000_000
 LATE_COST = 40_000_000_000
 ADD_LIMIT = 12 << 20
+GATED = False
 
 MU_A = 0.25 * NU_INF
 MU_B = 0.25 * (NU_ZERO - NU_INF)
@@ -181,7 +182,7 @@
 
 
 def early_kernel(
-    core_ref, inflow_ref, flow_ref, adj_ref, halo_ref, density_hbm, mask_hbm, labels_hbm,
+    core_ref, inflow_ref, flow_ref, adj_ref, near_ref, density_hbm, mask_hbm, labels_hbm,
     flow_out, adj_out, tx_out, fx_out,
     out_f, out_a, density_ref, mask_ref, labels_ref, w, tx, fx, ty, fy, sems, cell_sems, out_sems,
 ):
@@ -195,9 +196,10 @@
         for source, base, last in ((flow_ref, 0, 6), (adj_ref, 3, 7)):
             copies.append((source.at[i, 0:3], w.at[i, base : base + 3, 2:6, data, :]))
             copies.append((source.at[i, 3], w.at[i, last, 2:6, data, :]))
-        for c in range(6):
-            copies.append((halo_ref.at[i, 2 * c : 2 * c + 2], w.at[i, c, pl.ds(6 - 6 * core, 2), data, :]))
-        copies.append((halo_ref.at[i, 12:14], w.at[i, 6:8, 6 - 5 * core, data, :]))
+        for n in range(2):
+            for j in range(3):
+                copies.append((near_ref.at[i, n, 2 * j : 2 * j + 2], w.at[i, 3 * n + j, pl.ds(6 - 6 * core, 2), data, :]))
+            copies.append((near_ref.at[i, n, 6], w.at[i, 6 + n, 6 - 5 * core, data, :]))
         reads.append([pltpu.make_async_copy(a, b, sems.at[i, k]) for k, (a, b) in enumerate(copies)])
         copies = [(a.at[i, :, three], b.at[i, :, three]) for a, b in ((out_f, flow_out), (out_a, adj_out))]
         copies += [(a.at[i, :, 3:5], b.at[i]) for a, b in ((tx, tx_out), (fx, fx_out))]
@@ -232,60 +234,114 @@
             h.wait()
 
 
-def late_kernel(
-    core_ref, inflow_ref, flow_ref, adj_ref, far_ref, last_ref, density_hbm, mask_hbm, labels_hbm,
-    flow_part, adj_part, tx_part, fx_part, flow_out, adj_out,
-    out_f, out_a, density_ref, mask_ref, labels_ref, w, tx, fx, ty, fy, sems, part_sems, cell_sems, out_sems,
-):
+def late_kernel(core_ref, inflow_ref, flow_ref, adj_ref, far_ref, *refs):
+    cells_hbm, (_, _, tx_part, fx_part, flow_out, adj_out, sent), refs = refs[:3], refs[3:10], refs[10:]
+    out_f, out_a, density_ref, mask_ref, labels_ref, w, tx, fx, ty, fy, sems, part_sems, cell_sems, out_sems = refs
     insts = out_f.shape[0]
     core = core_ref[0]
+    at_end = inflow_ref[insts]
     data = pl.ds(TOP, ROWS)
+    pair, partial, own = pl.ds(2 * core, 2), pl.ds(1 + core, 1), pl.ds(2 + 2 * core, 2)
+    edge, last = 2 + 3 * core, 3 * core
     reads, parts, writes = [], [], []
-    pair, partial = pl.ds(2 * core, 2), pl.ds(1 + core, 1)
     for i in range(insts):
         copies = []
-        for source, base, last in ((flow_ref, 0, 6), (adj_ref, 3, 7)):
-            copies.append((source.at[i, 0:3, pair], w.at[i, base : base + 3, pl.ds(2 + 2 * core, 2), data, :]))
-            copies.append((source.at[i, 3, pair], w.at[i, last, pl.ds(2 + 2 * core, 2), data, :]))
-        cut = far_ref.shape[0]
-        halo_ref = far_ref.at[i] if i < cut else last_ref.at[i - cut]
-        for c in range(6):
-            copies.append((halo_ref.at[2 * c : 2 * c + 2], w.at[i, c, pl.ds(6 * core, 2), data, :]))
-        copies.append((halo_ref.at[12:14], w.at[i, 6:8, 1 + 5 * core, data, :]))
+        for n, source in enumerate((flow_ref, adj_ref)):
+            vel = slice(3 * n, 3 * n + 3)
+            copies.append((source.at[i, 0:3, pair], w.at[i, vel, own, data, :]))
+            copies.append((source.at[i, 3, pair], w.at[i, 6 + n, own, data, :]))
+            copies.append((far_ref.at[i, n], w.at[i, vel, 1 + 5 * core, data, :]))
         reads.append([pltpu.make_async_copy(a, b, sems.at[i, k]) for k, (a, b) in enumerate(copies)])
         copies = [(a.at[i, :, partial], b.at[i, :, partial]) for a, b in ((flow_out, out_f), (adj_out, out_a))]
         copies += [(a.at[i], b.at[i, :, 3:5]) for a, b in ((tx_part, tx), (fx_part, fx))]
         parts.append([pltpu.make_async_copy(a, b, part_sems.at[i, k]) for k, (a, b) in enumerate(copies)])
-        copies = ((out_f, flow_out), (out_a, adj_out))
-        writes.append([pltpu.make_async_copy(a.at[i, :, pair], b.at[i, :, pair], out_sems.at[i, k]) for k, (a, b) in enumerate(copies)])
-    cells = ((density_hbm, density_ref), (mask_hbm, mask_ref), (labels_hbm, labels_ref))
-    reads[0] += [
-        pltpu.make_async_copy(a.at[pl.ds(3 * core, 1)], b.at[pl.ds(3 * core, 1)], cell_sems.at[k])
-        for k, (a, b) in enumerate(cells)
-    ]
+        copies = [(a.at[i, :, edge], sent.at[i, n]) for n, a in enumerate((tx, fx))]
+        copies += [(a.at[i, :, pair], b.at[i, :, pair]) for a, b in ((out_f, flow_out), (out_a, adj_out))]
+        writes.append([pltpu.make_async_copy(a, b, out_sems.at[i, k]) for k, (a, b) in enumerate(copies)])
+    here = pl.ds(last, 1)
+    cells = zip(cells_hbm, (density_ref, mask_ref, labels_ref))
+    reads[0] += [pltpu.make_async_copy(a.at[here], b.at[here], cell_sems.at[k]) for k, (a, b) in enumerate(cells)]
     for i in range(insts):
         for h in reads[i] + parts[i]:
             h.start()
     for i in range(insts):
-        clear_edges(w, i, 4 * core, 4)
+        clear_edges(w, i, 1 + 3 * core, 3)
     tile_work, y_edges, collect, over = stencil_tools(
         inflow_ref, w, tx, fx, ty, fy, out_f, out_a, density_ref, mask_ref, labels_ref
     )
+    sign = at_end * (1.0 - 2.0 * core.astype(jnp.float32))
+
+    def beyond(i, t):
+        r = pl.multiple_of(t * TILE, 8)
+        here = pl.ds(r + TOP, TILE)
+        u = [w[i, j, edge, here, :] for j in range(3)]
+        lam = [w[i, 3 + j, edge, here, :] for j in range(3)]
+        outer_t, outer_f = outer_cell(u, lam, 0)
+        for j in range(3):
+            tx[i, j, 1 + 5 * core, pl.ds(r, TILE), :] = sign * outer_t[j]
+            fx[i, j, 1 + 5 * core, pl.ds(r, TILE), :] = sign * outer_f[j]
+
     for i in range(insts):
         for h in reads[i]:
             h.wait()
-        over(1 + 5 * core, 1, lambda p, t: tile_work(i, p, t, False))
-        over(2 + 3 * core, 1, lambda p, t: tile_work(i, p, t, True))
-        y_edges(i, 3 * core)
+        over(edge, 1, lambda p, t: tile_work(i, p, t, True))
+        for h in writes[i][:2]:
+            h.start()
+        y_edges(i, last)
+        over(edge, 1, lambda p, t: beyond(i, t))
         for h in parts[i]:
             h.wait()
-        over(2 + 3 * core, 1, lambda p, t: collect(i, p, t, True, True))
+        over(edge, 1, lambda p, t: collect(i, p, t, True, True))
         over(3 + core, 1, lambda p, t: collect(i, p, t, True, False))
-        for h in writes[i]:
+        for h in writes[i][2:]:
             h.start()
     for group in writes:
         for h in group:
             h.wait()
+
+
+def flux_kernel(core_ref, f_ref, a_ref, flux_hbm, out_f, out_a, total, flux, sems):
+    insts = out_f.shape[0]
+    core = core_ref[0]
+    sign = 1.0 - 2.0 * core.astype(jnp.float32)
+    work = [(i, n) for i in range(insts) for n in range(2)]
+    reads, writes = [], []
+    for k, (i, n) in enumerate(work):
+        out = (out_f, out_a)[n].at[i, 0:3, 3 * core]
+        reads.append(
+            (
+                pltpu.make_async_copy(out, total.at[i, n], sems.at[0, k]),
+                pltpu.make_async_copy(flux_hbm.at[i, n], flux.at[i, n], sems.at[1, k]),
+            )
+        )
+        writes.append(pltpu.make_async_copy(total.at[i, n], out, sems.at[2, k]))
+    for read in reads:
+        for h in read:
+            h.start()
+    for (i, n), read, write in zip(work, reads, writes):
+        for h in read:
+            h.wait()
+        total[i, n] = total[i, n] + sign * flux[i, n]
+        write.start()
+    for write in writes:
+        write.wait()
+
+
+def add_flux(core, flow_part, adj_part, flux):
+    space = pl.BlockSpec(memory_space=pltpu.HBM)
+    shape = jax.ShapeDtypeStruct(flow_part.shape, jnp.float32)
+    return pl.pallas_call(
+        flux_kernel,
+        out_shape=(shape, shape),
+        in_specs=[pl.BlockSpec(memory_space=pltpu.SMEM)] + [space] * 3,
+        out_specs=[space] * 2,
+        scratch_shapes=[pltpu.VMEM(flux.shape, jnp.float32)] * 2
+        + [pltpu.SemaphoreType.DMA((3, 2 * flow_part.shape[0]))],
+        compiler_params=pltpu.CompilerParams(vmem_limit_bytes=VMEM_LIMIT),
+        cost_estimate=pl.CostEstimate(flops=LATE_COST, bytes_accessed=8_000_000, transcendentals=0),
+        input_output_aliases={1: 0, 2: 1},
+        name="add_flux",
+    )(core, flow_part, adj_part, flux)
 
 
 def add_kernel(f_ref, a_ref, times, out_f, out_a, total, sems):
@@ -344,7 +400,7 @@
         + [pltpu.VMEM((insts, 8, 8, PADDED, LANES), jnp.float32)]
         + [pltpu.VMEM((insts, 3, 8, ROWS, LANES), jnp.float32)] * 2
         + [pltpu.VMEM((3, PLANES, PADDED, LANES), jnp.float32)] * 2
-        + [pltpu.SemaphoreType.DMA((insts, 11))]
+        + [pltpu.SemaphoreType.DMA((insts, 12))]
         + ([pltpu.SemaphoreType.DMA((insts, 4))] if late else [])
         + [pltpu.SemaphoreType.DMA((3,)), pltpu.SemaphoreType.DMA((insts, 4))],
         compiler_params=pltpu.CompilerParams(vmem_limit_bytes=VMEM_LIMIT),
@@ -399,14 +455,9 @@
     return b // 2, slice(b % 2 * half, (b % 2 + 1) * half)
 
 
-def halo_copies(flow_ref, adj_ref, ref, insts, first, near):
-    copies = []
-    for j in range(3):
-        copies.append((flow_ref.at[insts, j, pl.ds(first, 2)], ref.at[:, 2 * j : 2 * j + 2]))
-        copies.append((adj_ref.at[insts, j, pl.ds(first, 2)], ref.at[:, 6 + 2 * j : 8 + 2 * j]))
-    copies.append((flow_ref.at[insts, 3, pl.ds(near, 1)], ref.at[:, 12:13]))
-    copies.append((adj_ref.at[insts, 3, pl.ds(near, 1)], ref.at[:, 13:14]))
-    return copies
+def halo_copies(state_ref, ref, first, near):
+    copies = [(state_ref.at[:, j, pl.ds(first, 2)], ref.at[:, 2 * j : 2 * j + 2]) for j in range(3)]
+    return copies + [(state_ref.at[:, 3, pl.ds(near, 1)], ref.at[:, 6:7])]
 
 
 def block_copies(flow_ref, adj_ref, ref, b):
@@ -430,33 +481,39 @@
         write.wait()
 
 
-def pack_halo_kernel(core_ref, flow_ref, adj_ref, far_ref, last_ref, near_ref, far, last, near, sems):
+def pack_kernel(core_ref, flow_ref, adj_ref, blocks_ref, near_ref, far_ref, blocks, near, far, sems):
     core = core_ref[0]
-    insts = flow_ref.shape[0]
-    cut = far.shape[0]
-    groups = [(halo_copies(flow_ref, adj_ref, near, slice(0, insts), 2 - 2 * core, 3 - 3 * core), (near, near_ref))]
-    for ref, out, which in ((far, far_ref, slice(0, cut)), (last, last_ref, slice(cut, insts))):
-        groups.append((halo_copies(flow_ref, adj_ref, ref, which, 2 * core, 3 * core), (ref, out)))
-    through_vmem(groups, sems)
-
-
-def pack_block_kernel(core_ref, flow_ref, adj_ref, blocks_ref, blocks, sems):
-    groups = [
-        (block_copies(flow_ref, adj_ref, blocks, b), (blocks.at[b], blocks_ref.at[b])) for b in range(2 * PLANES)
-    ]
-    through_vmem(groups, sems)
-
-
-def pack(kernel, name, core, flow, adj, shapes):
+    states = (flow_ref, adj_ref)
+    copies = sum([halo_copies(state, near.at[:, n], 2 - 2 * core, 3 - 3 * core) for n, state in enumerate(states)], [])
+    halos = [(copies, (near, near_ref))]
+    copies = [(state.at[:, 0:3, 3 * core], far.at[:, n]) for n, state in enumerate(states)]
+    halos.append((copies, (far, far_ref)))
+    groups = []
+    for b in range(2 * PLANES):
+        groups.append((block_copies(flow_ref, adj_ref, blocks, b), (blocks.at[b], blocks_ref.at[b])))
+    through_vmem(halos + groups, sems)
+
+
+def pack(core, flow, adj):
+    insts = flow.shape[0]
     space = pl.BlockSpec(memory_space=pltpu.HBM)
+    halo = (insts, 2, 7, ROWS, LANES)
+    blocks = (2 * PLANES, insts, 6, ROWS // 2, LANES)
+    shapes = [blocks, halo, (insts, 2, 3, ROWS, LANES)]
+    copies = 8 + 1 + 2 + 1 + 6 * PLANES
     return pl.pallas_call(
-        kernel,
+        pack_kernel,
         out_shape=[jax.ShapeDtypeStruct(s, jnp.float32) for s in shapes],
         in_specs=[pl.BlockSpec(memory_space=pltpu.SMEM)] + [space] * 2,
         out_specs=[space] * len(shapes),
-        scratch_shapes=[pltpu.VMEM(s, jnp.float32) for s in shapes] + [pltpu.SemaphoreType.DMA((7 * PLANES,))],
+        scratch_shapes=[
+            pltpu.VMEM(blocks, jnp.float32),
+            pltpu.VMEM(halo, jnp.float32),
+            pltpu.VMEM(shapes[2], jnp.float32),
+            pltpu.SemaphoreType.DMA((copies,)),
+        ],
         compiler_params=pltpu.CompilerParams(vmem_limit_bytes=VMEM_LIMIT),
-        name=name,
+        name="pack",
     )(core, flow, adj)
 
 
@@ -467,27 +524,30 @@
     inflow = 1.0 + 0.5 * jnp.sin(2.0 * jnp.pi * instances.astype(jnp.float32) / NT)
 
     core = lax.axis_index("space") % 2
+    at_end = (lax.axis_index("space") == 0) | (lax.axis_index("space") == count - 1)
     core = core.reshape(1)
-    halo = (insts, 14, ROWS, LANES)
-    cut = insts // 2
-    halves = [(cut,) + halo[1:], (insts - cut,) + halo[1:]]
-    far, last, near = pack(pack_halo_kernel, "pack_halo", core, flow, adj, halves + [halo])
+    scalars = jnp.append(inflow, at_end.astype(jnp.float32))
+    blocks, near, far = pack(core, flow, adj)
+    near = lax.ppermute(near, "space", [p for i in range(0, count, 2) for p in ((i, i + 1), (i + 1, i))])
     across = [p for i in range(1, count - 1, 2) for p in ((i, i + 1), (i + 1, i))]
-    far, last = lax.ppermute(far, "space", across), lax.ppermute(last, "space", across)
-    near = lax.ppermute(near, "space", [p for i in range(0, count, 2) for p in ((i, i + 1), (i + 1, i))])
-    (blocks,) = pack(pack_block_kernel, "pack_block", core, flow, adj, [(2 * PLANES, insts, 6, ROWS // 2, LANES)])
+    far = lax.ppermute(far, "space", across)
+    if GATED:
+        blocks, near = lax.optimization_barrier((blocks, near))
     gathered = lax.all_to_all(blocks, "tm", 0, 0, tiled=True)
     cells = (density, mask, labels)
     edge = (insts, 3, 2, ROWS, LANES)
     parts = stencil(
-        early_kernel, "early", EARLY_COST, [flow.shape] * 2 + [edge] * 2, core, inflow, flow, adj, [near], cells
+        early_kernel, "early", EARLY_COST, [flow.shape] * 2 + [edge] * 2, core, scalars, flow, adj, [near], cells
     )
+    shapes = [flow.shape] * 2 + [(insts, 2, 3, ROWS, LANES)]
+    *parts, flux = stencil(late_kernel, "late", LATE_COST, shapes, core, scalars, flow, adj, [far], cells, *parts)
+    flux = lax.ppermute(flux, "space", across)
     gathered, *parts = lax.optimization_barrier((gathered, *parts))
     by_time = (NT,) + blocks.shape[2:]
     derived = time_derivative(gathered.reshape(by_time), blocks.reshape(by_time))
     time_part = lax.all_to_all(derived.reshape(blocks.shape), "tm", 0, 0, tiled=True)
-    late = stencil(late_kernel, "late", LATE_COST, [flow.shape] * 2, core, inflow, flow, adj, [far, last], cells, *parts)
-    return add_time(*late, time_part)
+    parts = add_flux(core, *parts, flux)
+    return add_time(*parts, time_part)
 
 
 def solution(mesh):

time: 74.9 us -> 71.8 us (0.959)
  the two profiles are of different devices: /device:TPU:13 before, /device:TPU:17 now
where the time goes in v2:
time: 71.8 us; the launch traced here: 71.4 us
  starting transfers between devices  23.9 us (33%)
  waiting for transfers between devices  22.2 us (31%)
  Pallas kernels  21.5 us (30%)
  local copies, waits for them, and re-layouts  2.39 us (3%)
  between operations  0.72 us (1%)
    all_to_all x1, waiting for transfers between devices, on_device(): lax.all_to_all(derived.reshape(blocks.shape), 'tm', 0, 0, tiled=True)  15 us
    pallas_call x2, Pallas kernels, stencil(): pl.pallas_call(kernel, out_shape=[jax.ShapeDtypeStruct(s, jnp.float32) fo...  12.4 us
    all_to_all x1, starting transfers between devices, on_device(): lax.all_to_all(derived.reshape(blocks.shape), 'tm', 0, 0, tiled=True)  8.38 us
    ppermute x1, waiting for transfers between devices, on_device(): far = lax.ppermute(far, 'space', across)  6.85 us
    ppermute x1, starting transfers between devices, on_device(): far = lax.ppermute(far, 'space', across)  5.4 us
    ppermute x1, starting transfers between devices, on_device(): flux = lax.ppermute(flux, 'space', across)  4.88 us
    all_to_all x1, starting transfers between devices, on_device(): gathered = lax.all_to_all(blocks, 'tm', 0, 0, tiled=True)  4.49 us
    pallas_call x1, Pallas kernels, pack(): pl.pallas_call(pack_kernel, out_shape=[jax.ShapeDtypeStruct(s, jnp.float3...  3.12 us
  transfers between devices with their start and end apart: 5, of which 3 were waited for; matrix products, arithmetic and copies ran while one was open for 1% of the time, Pallas kernels for 23%

profile of v2, /device:TPU:17, one launch (start us, length us, event | category | flops | bytes accessed | tf_op | source)
XLA Modules:
  0.0 71.4 jit_solution(11654402568102072209)
XLA Ops:
  0.6 3.1 %pack.1 = (f32[8,2,6,32,128]{4,3,2,1,0:T(8,128)}, f32[2,2,7,64,128]{4,3,2,1,0:T(8,128)}, f32[2,2,3,64,128]{4,3,2,1,0:T(8,128)}) custom-call(s32[1]{0:T(128)} %bitcast.core_ref, f32[2,4,4,64,128]{4,3,2,1,0:T(8,128)} %flow_ref.5, f32[2,4,4,64,128]{4,3,2,1,0:T(8,128)} %adj_ref.5), custom_call_target="tpu_custom_call" | custom-call | tf_op jit(solution)/shard_map/pack/pallas_call | solution.py:504
  3.8 0.8 %collective-permute-start.1 = (f32[2,2,7,64,128]{4,3,2,1,0:T(8,128)}, f32[2,2,7,64,128]{4,3,2,1,0:T(8,128)S(1)}, u32[]{:S(2)}, u32[]{:S(2)}) collective-permute-start(f32[2,2,7,64,128]{4,3,2,1,0:T(8,128)} %get-tuple-element.19), channel_id=1, source_target_pairs={{0,1},{1,0},{2,3},{3,2},{4,5},{5,4},{6,7},{7,6},{8,9},{9,8},{10,11... | collective-permute-start | bytes 2752520 | tf_op jit(solution)/shard_map/ppermute | solution.py:531
  4.5 5.4 %collective-permute-start = (f32[2,2,3,64,128]{4,3,2,1,0:T(8,128)}, f32[2,2,3,64,128]{4,3,2,1,0:T(8,128)S(1)}, u32[]{:S(2)}, u32[]{:S(2)}) collective-permute-start(f32[2,2,3,64,128]{4,3,2,1,0:T(8,128)} %get-tuple-element.18), channel_id=1, source_target_pairs={{1,2},{2,1},{3,4},{4,3},{5,6},{6,5},{7,8},{8,7},{9,10},{10,9},{11,... | collective-permute-start | bytes 1179656 | tf_op jit(solution)/shard_map/ppermute | solution.py:533
  9.9 4.5 %all-to-all-start = ((f32[8,2,6,32,128]{4,3,2,1,0:T(8,128)}), f32[8,2,6,32,128]{4,3,2,1,0:T(8,128)S(1)}, u32[]{:S(2)}, u32[]{:S(2)}) async-start(f32[8,2,6,32,128]{4,3,2,1,0:T(8,128)} %get-tuple-element.17), calls=%async_computation | async-start | bytes 3145728 | tf_op jit(solution)/shard_map/all_to_all | solution.py:536
  14.5 0.7 pad_maximum_fusion.inflow_ref
  15.1 0.0 collective-permute-done.1.near_ref
  15.1 0.0 copy-start
  15.1 0.9 %copy-done = f32[2,2,7,64,128]{4,3,2,1,0:T(8,128)} copy-done((f32[2,2,7,64,128]{4,3,2,1,0:T(8,128)}, f32[2,2,7,64,128]{4,3,2,1,0:T(8,128)S(1)}, u32[]{:S(2)}) %copy-start) | copy-done | bytes 917528
  16.1 7.7 %early.1 = (f32[2,4,4,64,128]{4,3,2,1,0:T(8,128)}, f32[2,4,4,64,128]{4,3,2,1,0:T(8,128)}, f32[2,3,2,64,128]{4,3,2,1,0:T(8,128)}, f32[2,3,2,64,128]{4,3,2,1,0:T(8,128)}) custom-call(s32[1]{0:T(128)} %bitcast.core_ref, f32[3]{0:T(128)} %pad_maximum_fusion.inflow_ref, f32[2,4,4,64,128]{4,3,2,1,0:T(8,128)} %flow_ref.5, f32[2,4,4,64,128]{4,3,2,1,0:T(8,128)} %adj_ref.5, ...), custom_call_target="tpu_custom_call" | custom-call | flops 20000000000 | bytes 8000000 | tf_op jit(solution)/shard_map/early/pallas_call | solution.py:393
  23.7 6.8 %collective-permute-done.far_ref = f32[2,2,3,64,128]{4,3,2,1,0:T(8,128)S(1)} collective-permute-done((f32[2,2,3,64,128]{4,3,2,1,0:T(8,128)}, f32[2,2,3,64,128]{4,3,2,1,0:T(8,128)S(1)}, u32[]{:S(2)}, u32[]{:S(2)}) %collective-permute-start) | collective-permute-done | bytes 393248 | tf_op jit(solution)/shard_map/ppermute | solution.py:533
  30.6 0.0 copy-start.1
  30.6 0.7 %copy-done.1 = f32[2,2,3,64,128]{4,3,2,1,0:T(8,128)} copy-done((f32[2,2,3,64,128]{4,3,2,1,0:T(8,128)}, f32[2,2,3,64,128]{4,3,2,1,0:T(8,128)S(1)}, u32[]{:S(2)}) %copy-start.1) | copy-done | bytes 393240
  31.3 4.7 %late.1 = (f32[2,4,4,64,128]{4,3,2,1,0:T(8,128)}, f32[2,4,4,64,128]{4,3,2,1,0:T(8,128)}, f32[2,2,3,64,128]{4,3,2,1,0:T(8,128)}) custom-call(s32[1]{0:T(128)} %bitcast.core_ref, f32[3]{0:T(128)} %pad_maximum_fusion.inflow_ref, f32[2,4,4,64,128]{4,3,2,1,0:T(8,128)} %flow_ref.5, ...), custom_call_target="tpu_custom_call", output_to_operand_aliasing={{0}: (8, {}), {1}: (9, {})} | custom-call | flops 40000000000 | bytes 8000000 | tf_op jit(solution)/shard_map/late/pallas_call | solution.py:393
  36.1 4.9 %collective-permute-start.2 = (f32[2,2,3,64,128]{4,3,2,1,0:T(8,128)}, f32[2,2,3,64,128]{4,3,2,1,0:T(8,128)S(1)}, u32[]{:S(2)}, u32[]{:S(2)}) collective-permute-start(f32[2,2,3,64,128]{4,3,2,1,0:T(8,128)} %get-tuple-element.28), channel_id=1, source_target_pairs={{1,2},{2,1},{3,4},{4,3},{5,6},{6,5},{7,8},{8,7},{9,10},{10,9},{11,... | collective-permute-start | bytes 1179656 | tf_op jit(solution)/shard_map/ppermute | solution.py:544
  41.0 0.3 all-to-all-done
  41.3 1.7 %time_derivative.1 = f32[16,6,32,128]{3,2,1,0:T(8,128)} custom-call(f32[16,6,32,128]{3,2,1,0:T(8,128)S(1)} %bitcast.5, f32[16,6,32,128]{3,2,1,0:T(8,128)} %bitcast.3.sent_hbm), custom_call_target="tpu_custom_call", output_to_operand_aliasing={{}: (1, {})} | custom-call | flops 12000000 | bytes 3200000 | tf_op jit(solution)/shard_map/time_derivative/pallas_call | solution.py:440
  43.0 8.4 %all-to-all-start.1 = ((f32[8,2,6,32,128]{4,3,2,1,0:T(8,128)}), f32[8,2,6,32,128]{4,3,2,1,0:T(8,128)S(1)}, u32[]{:S(2)}, u32[]{:S(2)}) async-start(f32[8,2,6,32,128]{4,3,2,1,0:T(8,128)} %bitcast.4), calls=%async_computation.1 | async-start | bytes 3145728 | tf_op jit(solution)/shard_map/all_to_all | solution.py:548
  51.4 0.0 collective-permute-done.2.flux_hbm
  51.4 0.0 copy-start.2
  51.4 0.7 %copy-done.2 = f32[2,2,3,64,128]{4,3,2,1,0:T(8,128)} copy-done((f32[2,2,3,64,128]{4,3,2,1,0:T(8,128)}, f32[2,2,3,64,128]{4,3,2,1,0:T(8,128)S(1)}, u32[]{:S(2)}) %copy-start.2) | copy-done | bytes 393240
  52.2 2.0 %add_flux.1 = (f32[2,4,4,64,128]{4,3,2,1,0:T(8,128)}, f32[2,4,4,64,128]{4,3,2,1,0:T(8,128)}) custom-call(s32[1]{0:T(128)} %bitcast.core_ref, f32[2,4,4,64,128]{4,3,2,1,0:T(8,128)} %get-tuple-element.26.f_ref, f32[2,4,4,64,128]{4,3,2,1,0:T(8,128)} %get-tuple-element.27.a_ref, ...), custom_call_target="tpu_custom_call", output_to_operand_aliasing={{0}: (1, {}), {1}: (2, {})} | custom-call | flops 40000000000 | bytes 8000000 | tf_op jit(solution)/shard_map/add_flux/pallas_call | solution.py:333
  54.1 15.0 %all-to-all-done.1.times = f32[8,2,6,32,128]{4,3,2,1,0:T(8,128)S(1)} async-done(((f32[8,2,6,32,128]{4,3,2,1,0:T(8,128)}), f32[8,2,6,32,128]{4,3,2,1,0:T(8,128)S(1)}, u32[]{:S(2)}, u32[]{:S(2)}) %all-to-all-start.1) | async-done | bytes 1572896 | tf_op jit(solution)/shard_map/all_to_all | solution.py:548
  69.1 2.2 %add_time.1 = (f32[2,4,4,64,128]{4,3,2,1,0:T(8,128)}, f32[2,4,4,64,128]{4,3,2,1,0:T(8,128)}) custom-call(f32[2,4,4,64,128]{4,3,2,1,0:T(8,128)} %get-tuple-element.29.f_ref, f32[2,4,4,64,128]{4,3,2,1,0:T(8,128)} %get-tuple-element.30.a_ref, f32[8,2,6,32,128]{4,3,2,1,0:T(8,128)S(1)} %all-to-all-done.1.times), custom_call_target="tpu_custom_call", output_to_operand_aliasing={{0}: (0, {}), {1}: (1, {})} | custom-call | tf_op jit(solution)/shard_map/add_time/pallas_call | solution.py:372
  (1 shorter events, 0.0 us)
Async XLA Ops:
  3.8 11.4 %collective-permute-start.1 = (f32[2,2,7,64,128]{4,3,2,1,0:T(8,128)}, f32[2,2,7,64,128]{4,3,2,1,0:T(8,128)S(1)}, u32[]{:S(2)}, u32[]{:S(2)}) collective-permute-start(f32[2,2,7,64,128]{4,3,2,1,0:T(8,128)} %get-tuple-element.19), channel_id=1, source_target_pairs={{0,1},{1,0},{2,3},{3,2},{4,5},{5,4},{6,7},{7,6},{8,9},{9,8},{10,11... | collective-permute-start | bytes 2752520 | tf_op jit(solution)/shard_map/ppermute | solution.py:531
  4.5 26.1 %collective-permute-start = (f32[2,2,3,64,128]{4,3,2,1,0:T(8,128)}, f32[2,2,3,64,128]{4,3,2,1,0:T(8,128)S(1)}, u32[]{:S(2)}, u32[]{:S(2)}) collective-permute-start(f32[2,2,3,64,128]{4,3,2,1,0:T(8,128)} %get-tuple-element.18), channel_id=1, source_target_pairs={{1,2},{2,1},{3,4},{4,3},{5,6},{6,5},{7,8},{8,7},{9,10},{10,9},{11,... | collective-permute-start | bytes 1179656 | tf_op jit(solution)/shard_map/ppermute | solution.py:533
  9.9 31.4 %all-to-all-start = ((f32[8,2,6,32,128]{4,3,2,1,0:T(8,128)}), f32[8,2,6,32,128]{4,3,2,1,0:T(8,128)S(1)}, u32[]{:S(2)}, u32[]{:S(2)}) async-start(f32[8,2,6,32,128]{4,3,2,1,0:T(8,128)} %get-tuple-element.17), calls=%async_computation | async-start | bytes 3145728 | tf_op jit(solution)/shard_map/all_to_all | solution.py:536
  15.1 0.9 %copy-start = (f32[2,2,7,64,128]{4,3,2,1,0:T(8,128)}, f32[2,2,7,64,128]{4,3,2,1,0:T(8,128)S(1)}, u32[]{:S(2)}) copy-start(f32[2,2,7,64,128]{4,3,2,1,0:T(8,128)S(1)} %collective-permute-done.1.near_ref) | copy-start | bytes 2752516
  30.6 0.7 %copy-start.1 = (f32[2,2,3,64,128]{4,3,2,1,0:T(8,128)}, f32[2,2,3,64,128]{4,3,2,1,0:T(8,128)S(1)}, u32[]{:S(2)}) copy-start(f32[2,2,3,64,128]{4,3,2,1,0:T(8,128)S(1)} %collective-permute-done.far_ref) | copy-start | bytes 1179652
  36.1 15.4 %collective-permute-start.2 = (f32[2,2,3,64,128]{4,3,2,1,0:T(8,128)}, f32[2,2,3,64,128]{4,3,2,1,0:T(8,128)S(1)}, u32[]{:S(2)}, u32[]{:S(2)}) collective-permute-start(f32[2,2,3,64,128]{4,3,2,1,0:T(8,128)} %get-tuple-element.28), channel_id=1, source_target_pairs={{1,2},{2,1},{3,4},{4,3},{5,6},{6,5},{7,8},{8,7},{9,10},{10,9},{11,... | collective-permute-start | bytes 1179656 | tf_op jit(solution)/shard_map/ppermute | solution.py:544
  43.0 26.1 %all-to-all-start.1 = ((f32[8,2,6,32,128]{4,3,2,1,0:T(8,128)}), f32[8,2,6,32,128]{4,3,2,1,0:T(8,128)S(1)}, u32[]{:S(2)}, u32[]{:S(2)}) async-start(f32[8,2,6,32,128]{4,3,2,1,0:T(8,128)} %bitcast.4), calls=%async_computation.1 | async-start | bytes 3145728 | tf_op jit(solution)/shard_map/all_to_all | solution.py:548
  51.4 0.7 %copy-start.2 = (f32[2,2,3,64,128]{4,3,2,1,0:T(8,128)}, f32[2,2,3,64,128]{4,3,2,1,0:T(8,128)S(1)}, u32[]{:S(2)}) copy-start(f32[2,2,3,64,128]{4,3,2,1,0:T(8,128)S(1)} %collective-permute-done.2.flux_hbm) | copy-start | bytes 1179652

commit v3 on v2

--- a/solution.py
+++ b/solution.py
@@ -22,7 +22,7 @@
 LANES = 128
 TOP = 8
 PADDED = ROWS + 2 * TOP
-TILE = 16
+TILE = 32
 UNROLL = 2
 VMEM_LIMIT = 56 << 20
 EARLY_COST = 20_000_000_000
@@ -300,88 +300,82 @@
             h.wait()
 
 
-def flux_kernel(core_ref, f_ref, a_ref, flux_hbm, out_f, out_a, total, flux, sems):
-    insts = out_f.shape[0]
+def load_kernel(f_ref, a_ref, total, sems):
+    insts = f_ref.shape[0]
+    work = [(i, n) for i in range(insts) for n in range(2)]
+    reads = []
+    for k, (i, n) in enumerate(work):
+        reads.append(pltpu.make_async_copy((f_ref, a_ref)[n].at[i, 0:3], total.at[i, n], sems.at[k]))
+        reads[-1].start()
+    for read in reads:
+        read.wait()
+
+
+def load_parts(flow_part, adj_part):
+    insts = flow_part.shape[0]
+    return pl.pallas_call(
+        load_kernel,
+        out_shape=jax.ShapeDtypeStruct((insts, 2, 3) + flow_part.shape[2:], jnp.float32),
+        in_specs=[pl.BlockSpec(memory_space=pltpu.HBM)] * 2,
+        out_specs=pl.BlockSpec(memory_space=pltpu.VMEM),
+        scratch_shapes=[pltpu.SemaphoreType.DMA((2 * insts,))],
+        compiler_params=pltpu.CompilerParams(vmem_limit_bytes=ADD_LIMIT),
+        name="load_parts",
+    )(flow_part, adj_part)
+
+
+def flux_kernel(core_ref, part, flux, total):
     core = core_ref[0]
     sign = 1.0 - 2.0 * core.astype(jnp.float32)
-    work = [(i, n) for i in range(insts) for n in range(2)]
-    reads, writes = [], []
-    for k, (i, n) in enumerate(work):
-        out = (out_f, out_a)[n].at[i, 0:3, 3 * core]
-        reads.append(
-            (
-                pltpu.make_async_copy(out, total.at[i, n], sems.at[0, k]),
-                pltpu.make_async_copy(flux_hbm.at[i, n], flux.at[i, n], sems.at[1, k]),
-            )
-        )
-        writes.append(pltpu.make_async_copy(total.at[i, n], out, sems.at[2, k]))
-    for read in reads:
-        for h in read:
-            h.start()
-    for (i, n), read, write in zip(work, reads, writes):
-        for h in read:
-            h.wait()
-        total[i, n] = total[i, n] + sign * flux[i, n]
-        write.start()
+    for i in range(part.shape[0]):
+        for n in range(2):
+            total[i, n] = part[i, n]
+            total[i, n, :, 3 * core] = part[i, n, :, 3 * core] + sign * flux[i, n]
+
+
+def add_flux(core, part, flux):
+    whole = pl.BlockSpec(memory_space=pltpu.VMEM)
+    return pl.pallas_call(
+        flux_kernel,
+        out_shape=jax.ShapeDtypeStruct(part.shape, jnp.float32),
+        in_specs=[pl.BlockSpec(memory_space=pltpu.SMEM)] + [whole] * 2,
+        out_specs=whole,
+        compiler_params=pltpu.CompilerParams(vmem_limit_bytes=ADD_LIMIT),
+        cost_estimate=pl.CostEstimate(flops=LATE_COST, bytes_accessed=8_000_000, transcendentals=0),
+        name="add_flux",
+    )(core, part, flux)
+
+
+def add_kernel(f_ref, a_ref, part, times, out_f, out_a, total, sems):
+    insts = out_f.shape[0]
+    writes = []
+    for i in range(insts):
+        for n in range(2):
+            for j in range(3):
+                for b in range(2 * PLANES):
+                    q, rows = block_cells(b)
+                    total[i, n, j, q, rows, :] = part[i, n, j, q, rows, :] + times[b, i, 3 * n + j]
+                out = (out_f, out_a)[n].at[i, j]
+                writes.append(pltpu.make_async_copy(total.at[i, n, j], out, sems.at[len(writes)]))
+                writes[-1].start()
     for write in writes:
         write.wait()
 
 
-def add_flux(core, flow_part, adj_part, flux):
-    space = pl.BlockSpec(memory_space=pltpu.HBM)
-    shape = jax.ShapeDtypeStruct(flow_part.shape, jnp.float32)
-    return pl.pallas_call(
-        flux_kernel,
-        out_shape=(shape, shape),
-        in_specs=[pl.BlockSpec(memory_space=pltpu.SMEM)] + [space] * 3,
-        out_specs=[space] * 2,
-        scratch_shapes=[pltpu.VMEM(flux.shape, jnp.float32)] * 2
-        + [pltpu.SemaphoreType.DMA((3, 2 * flow_part.shape[0]))],
-        compiler_params=pltpu.CompilerParams(vmem_limit_bytes=VMEM_LIMIT),
-        cost_estimate=pl.CostEstimate(flops=LATE_COST, bytes_accessed=8_000_000, transcendentals=0),
-        input_output_aliases={1: 0, 2: 1},
-        name="add_flux",
-    )(core, flow_part, adj_part, flux)
-
-
-def add_kernel(f_ref, a_ref, times, out_f, out_a, total, sems):
-    insts = out_f.shape[0]
-    work = [(i, n) for i in range(insts) for n in range(2)]
-    reads, writes = [], []
-    for k, (i, n) in enumerate(work):
-        out = (out_f, out_a)[n].at[i, 0:3]
-        reads.append(pltpu.make_async_copy(out, total.at[i, n], sems.at[0, k]))
-        writes.append(pltpu.make_async_copy(total.at[i, n], out, sems.at[1, k]))
-    for read in reads:
-        read.start()
-    for (i, n), read, write in zip(work, reads, writes):
-        read.wait()
-        for j in range(3):
-            for b in range(2 * PLANES):
-                q, rows = block_cells(b)
-                total[i, n, j, q, rows, :] = total[i, n, j, q, rows, :] + times[b, i, 3 * n + j]
-        write.start()
-    for write in writes:
-        write.wait()
-
-
-def add_time(flow_part, adj_part, time_part):
+def add_time(flow_part, adj_part, part, time_part):
     space = pl.BlockSpec(memory_space=pltpu.HBM)
     insts = flow_part.shape[0]
     shape = jax.ShapeDtypeStruct(flow_part.shape, jnp.float32)
     return pl.pallas_call(
         add_kernel,
         out_shape=(shape, shape),
-        in_specs=[space] * 2 + [pl.BlockSpec(memory_space=pltpu.VMEM)],
+        in_specs=[space] * 2 + [pl.BlockSpec(memory_space=pltpu.VMEM)] * 2,
         out_specs=[space] * 2,
-        scratch_shapes=[
-            pltpu.VMEM((insts, 2, 3) + flow_part.shape[2:], jnp.float32),
-            pltpu.SemaphoreType.DMA((2, 2 * insts)),
-        ],
+        scratch_shapes=[pltpu.VMEM(part.shape, jnp.float32), pltpu.SemaphoreType.DMA((6 * insts,))],
         compiler_params=pltpu.CompilerParams(vmem_limit_bytes=ADD_LIMIT),
         input_output_aliases={0: 0, 1: 1},
         name="add_time",
-    )(flow_part, adj_part, time_part)
+    )(flow_part, adj_part, part, time_part)
 
 
 def stencil(kernel, name, cost, out_shapes, core, inflow, flow, adj, halos, cells, *parts):
@@ -430,7 +424,7 @@
                 out_ref[m + 8, c, rows, :] = -sum(coef[k - 1] * diff[7 - k] for k in range(1, 8))
             return 0
 
-        lax.fori_loop(0, tiles, step, 0, unroll=2)
+        lax.fori_loop(0, tiles, step, 0, unroll=4)
         writes[c].start()
     for h in writes:
         h.wait()
@@ -546,8 +540,7 @@
     by_time = (NT,) + blocks.shape[2:]
     derived = time_derivative(gathered.reshape(by_time), blocks.reshape(by_time))
     time_part = lax.all_to_all(derived.reshape(blocks.shape), "tm", 0, 0, tiled=True)
-    parts = add_flux(core, *parts, flux)
-    return add_time(*parts, time_part)
+    return add_time(*parts, add_flux(core, load_parts(*parts), flux), time_part)
 
 
 def solution(mesh):

time: 71.8 us -> 70.8 us (0.986)
  Pallas kernels: 21.5 us -> 18.2 us
  waiting for transfers between devices: 22.2 us -> 24.3 us
    pallas_call x2, Pallas kernels: 12.4 us -> 11.3 us  [stencil(): pl.pallas_call(kernel, out_shape=[jax.ShapeDtypeStruct(s, jnp.float32) fo...]
    pallas_call x1 -> x2, Pallas kernels: 1.97 us -> 0.93 us  [the longest x1 0.78 us: load_parts(): pl.pallas_call(load_kernel, out_shape=jax.ShapeDtypeStruct((insts, 2, 3)...]
    all_to_all x1, waiting for transfers between devices: 15 us -> 16 us  [on_device(): lax.all_to_all(derived.reshape(blocks.shape), 'tm', 0, 0, tiled=True)]
    pallas_call x1, Pallas kernels: 2.24 us -> 1.24 us  [add_time(): pl.pallas_call(add_kernel, out_shape=(shape, shape), in_specs=[space] * 2...]
    unnamed x6 -> x8, local copies, waits for them, and re-layouts: 2.39 us -> 2.89 us
  transfers between devices with their start and end apart: 5 -> 5, of which waited for: 3 -> 3; matrix products, arithmetic and copies ran while one was open for 1% -> 1% of each run, Pallas kernels for 23% -> 20%
where the time goes in v3:
time: 70.8 us; the launch traced here: 70.4 us
  waiting for transfers between devices  24.3 us (34%)
  starting transfers between devices  23.5 us (33%)
  Pallas kernels  18.2 us (26%)
  local copies, waits for them, and re-layouts  2.89 us (4%)
  between operations  0.74 us (1%)
  other arithmetic  0.71 us (1%)
    all_to_all x1, waiting for transfers between devices, on_device(): lax.all_to_all(derived.reshape(blocks.shape), 'tm', 0, 0, tiled=True)  16 us
    pallas_call x2, Pallas kernels, stencil(): pl.pallas_call(kernel, out_shape=[jax.ShapeDtypeStruct(s, jnp.float32) fo...  11.3 us
    all_to_all x1, starting transfers between devices, on_device(): lax.all_to_all(derived.reshape(blocks.shape), 'tm', 0, 0, tiled=True)  8.01 us
    ppermute x1, waiting for transfers between devices, on_device(): far = lax.ppermute(far, 'space', across)  7.53 us
    ppermute x1, starting transfers between devices, on_device(): far = lax.ppermute(far, 'space', across)  5.4 us
    ppermute x1, starting transfers between devices, on_device(): flux = lax.ppermute(flux, 'space', across)  4.84 us
    all_to_all x1, starting transfers between devices, on_device(): gathered = lax.all_to_all(blocks, 'tm', 0, 0, tiled=True)  4.49 us
    pallas_call x1, Pallas kernels, pack(): pl.pallas_call(pack_kernel, out_shape=[jax.ShapeDtypeStruct(s, jnp.float3...  3.12 us
  transfers between devices with their start and end apart: 5, of which 3 were waited for; matrix products, arithmetic and copies ran while one was open for 1% of the time, Pallas kernels for 20%

profile of v3, /device:TPU:17, one launch (start us, length us, event | category | flops | bytes accessed | tf_op | source)
XLA Modules:
  0.0 70.4 jit_solution(11864305407949916831)
XLA Ops:
  0.6 3.1 %pack.1 = (f32[8,2,6,32,128]{4,3,2,1,0:T(8,128)}, f32[2,2,7,64,128]{4,3,2,1,0:T(8,128)}, f32[2,2,3,64,128]{4,3,2,1,0:T(8,128)}) custom-call(s32[1]{0:T(128)} %bitcast.core_ref, f32[2,4,4,64,128]{4,3,2,1,0:T(8,128)} %flow_ref.5, f32[2,4,4,64,128]{4,3,2,1,0:T(8,128)} %adj_ref.5), custom_call_target="tpu_custom_call" | custom-call | tf_op jit(solution)/shard_map/pack/pallas_call | solution.py:498
  3.8 0.8 %collective-permute-start.1 = (f32[2,2,7,64,128]{4,3,2,1,0:T(8,128)}, f32[2,2,7,64,128]{4,3,2,1,0:T(8,128)S(1)}, u32[]{:S(2)}, u32[]{:S(2)}) collective-permute-start(f32[2,2,7,64,128]{4,3,2,1,0:T(8,128)} %get-tuple-element.17), channel_id=1, source_target_pairs={{0,1},{1,0},{2,3},{3,2},{4,5},{5,4},{6,7},{7,6},{8,9},{9,8},{10,11... | collective-permute-start | bytes 2752520 | tf_op jit(solution)/shard_map/ppermute | solution.py:525
  4.5 5.4 %collective-permute-start = (f32[2,2,3,64,128]{4,3,2,1,0:T(8,128)}, f32[2,2,3,64,128]{4,3,2,1,0:T(8,128)S(1)}, u32[]{:S(2)}, u32[]{:S(2)}) collective-permute-start(f32[2,2,3,64,128]{4,3,2,1,0:T(8,128)} %get-tuple-element.16), channel_id=1, source_target_pairs={{1,2},{2,1},{3,4},{4,3},{5,6},{6,5},{7,8},{8,7},{9,10},{10,9},{11,... | collective-permute-start | bytes 1179656 | tf_op jit(solution)/shard_map/ppermute | solution.py:527
  9.9 4.5 %all-to-all-start = ((f32[8,2,6,32,128]{4,3,2,1,0:T(8,128)}), f32[8,2,6,32,128]{4,3,2,1,0:T(8,128)S(1)}, u32[]{:S(2)}, u32[]{:S(2)}) async-start(f32[8,2,6,32,128]{4,3,2,1,0:T(8,128)} %get-tuple-element.15), calls=%async_computation | async-start | bytes 3145728 | tf_op jit(solution)/shard_map/all_to_all | solution.py:530
  14.5 0.7 pad_maximum_fusion.inflow_ref
  15.1 0.0 collective-permute-done.1.near_ref
  15.1 0.0 copy-start.2
  15.1 0.9 %copy-done.2 = f32[2,2,7,64,128]{4,3,2,1,0:T(8,128)} copy-done((f32[2,2,7,64,128]{4,3,2,1,0:T(8,128)}, f32[2,2,7,64,128]{4,3,2,1,0:T(8,128)S(1)}, u32[]{:S(2)}) %copy-start.2) | copy-done | bytes 917528
  16.1 7.0 %early.1 = (f32[2,4,4,64,128]{4,3,2,1,0:T(8,128)}, f32[2,4,4,64,128]{4,3,2,1,0:T(8,128)}, f32[2,3,2,64,128]{4,3,2,1,0:T(8,128)}, f32[2,3,2,64,128]{4,3,2,1,0:T(8,128)}) custom-call(s32[1]{0:T(128)} %bitcast.core_ref, f32[3]{0:T(128)} %pad_maximum_fusion.inflow_ref, f32[2,4,4,64,128]{4,3,2,1,0:T(8,128)} %flow_ref.5, f32[2,4,4,64,128]{4,3,2,1,0:T(8,128)} %adj_ref.5, ...), custom_call_target="tpu_custom_call" | custom-call | flops 20000000000 | bytes 8000000 | tf_op jit(solution)/shard_map/early/pallas_call | solution.py:387
  23.1 7.5 %collective-permute-done.far_ref = f32[2,2,3,64,128]{4,3,2,1,0:T(8,128)S(1)} collective-permute-done((f32[2,2,3,64,128]{4,3,2,1,0:T(8,128)}, f32[2,2,3,64,128]{4,3,2,1,0:T(8,128)S(1)}, u32[]{:S(2)}, u32[]{:S(2)}) %collective-permute-start) | collective-permute-done | bytes 393248 | tf_op jit(solution)/shard_map/ppermute | solution.py:527
  30.6 0.0 copy-start.3
  30.6 0.7 %copy-done.3 = f32[2,2,3,64,128]{4,3,2,1,0:T(8,128)} copy-done((f32[2,2,3,64,128]{4,3,2,1,0:T(8,128)}, f32[2,2,3,64,128]{4,3,2,1,0:T(8,128)S(1)}, u32[]{:S(2)}) %copy-start.3) | copy-done | bytes 393240
  31.3 4.3 %late.1 = (f32[2,4,4,64,128]{4,3,2,1,0:T(8,128)}, f32[2,4,4,64,128]{4,3,2,1,0:T(8,128)}, f32[2,2,3,64,128]{4,3,2,1,0:T(8,128)}) custom-call(s32[1]{0:T(128)} %bitcast.core_ref, f32[3]{0:T(128)} %pad_maximum_fusion.inflow_ref, f32[2,4,4,64,128]{4,3,2,1,0:T(8,128)} %flow_ref.5, ...), custom_call_target="tpu_custom_call", output_to_operand_aliasing={{0}: (8, {}), {1}: (9, {})} | custom-call | flops 40000000000 | bytes 8000000 | tf_op jit(solution)/shard_map/late/pallas_call | solution.py:387
  35.6 4.8 %collective-permute-start.2 = (f32[2,2,3,64,128]{4,3,2,1,0:T(8,128)}, f32[2,2,3,64,128]{4,3,2,1,0:T(8,128)S(1)}, u32[]{:S(2)}, u32[]{:S(2)}) collective-permute-start(f32[2,2,3,64,128]{4,3,2,1,0:T(8,128)} %get-tuple-element.26), channel_id=1, source_target_pairs={{1,2},{2,1},{3,4},{4,3},{5,6},{6,5},{7,8},{8,7},{9,10},{10,9},{11,... | collective-permute-start | bytes 1179656 | tf_op jit(solution)/shard_map/ppermute | solution.py:538
  40.5 0.8 %all-to-all-done = f32[8,2,6,32,128]{4,3,2,1,0:T(8,128)S(1)} async-done(((f32[8,2,6,32,128]{4,3,2,1,0:T(8,128)}), f32[8,2,6,32,128]{4,3,2,1,0:T(8,128)S(1)}, u32[]{:S(2)}, u32[]{:S(2)}) %all-to-all-start) | async-done | bytes 1572896 | tf_op jit(solution)/shard_map/all_to_all | solution.py:530
  41.3 1.6 %time_derivative.1 = f32[16,6,32,128]{3,2,1,0:T(8,128)} custom-call(f32[16,6,32,128]{3,2,1,0:T(8,128)S(1)} %bitcast.5, f32[16,6,32,128]{3,2,1,0:T(8,128)} %bitcast.3.sent_hbm), custom_call_target="tpu_custom_call", output_to_operand_aliasing={{}: (1, {})} | custom-call | flops 12000000 | bytes 3200000 | tf_op jit(solution)/shard_map/time_derivative/pallas_call | solution.py:434
  42.9 0.0 copy-start
  42.9 8.0 %all-to-all-start.1 = ((f32[8,2,6,32,128]{4,3,2,1,0:T(8,128)}), f32[8,2,6,32,128]{4,3,2,1,0:T(8,128)S(1)}, u32[]{:S(2)}, u32[]{:S(2)}) async-start(f32[8,2,6,32,128]{4,3,2,1,0:T(8,128)} %bitcast.4), calls=%async_computation.1 | async-start | bytes 3145728 | tf_op jit(solution)/shard_map/all_to_all | solution.py:542
  50.9 0.0 copy-done
  51.0 0.0 copy-start.1
  51.0 1.2 %copy-done.1 = f32[2,4,4,64,128]{4,3,2,1,0:T(8,128)S(1)} copy-done((f32[2,4,4,64,128]{4,3,2,1,0:T(8,128)S(1)}, f32[2,4,4,64,128]{4,3,2,1,0:T(8,128)}, u32[]{:S(2)}) %copy-start.1) | copy-done | bytes 1048600
  52.2 0.8 %load_parts.1.part = f32[2,2,3,4,64,128]{5,4,3,2,1,0:T(8,128)S(1)} custom-call(f32[2,4,4,64,128]{4,3,2,1,0:T(8,128)S(1)} %copy-done, f32[2,4,4,64,128]{4,3,2,1,0:T(8,128)S(1)} %copy-done.1), custom_call_target="tpu_custom_call" | custom-call | tf_op jit(solution)/shard_map/load_parts/pallas_call | solution.py:316
  53.0 0.0 collective-permute-done.2.flux
  53.0 0.1 add_flux.1.part
  53.1 16.0 %all-to-all-done.1.times = f32[8,2,6,32,128]{4,3,2,1,0:T(8,128)S(1)} async-done(((f32[8,2,6,32,128]{4,3,2,1,0:T(8,128)}), f32[8,2,6,32,128]{4,3,2,1,0:T(8,128)S(1)}, u32[]{:S(2)}, u32[]{:S(2)}) %all-to-all-start.1) | async-done | bytes 1572896 | tf_op jit(solution)/shard_map/all_to_all | solution.py:542
  69.1 1.2 %add_time.1 = (f32[2,4,4,64,128]{4,3,2,1,0:T(8,128)}, f32[2,4,4,64,128]{4,3,2,1,0:T(8,128)}) custom-call(f32[2,4,4,64,128]{4,3,2,1,0:T(8,128)} %get-tuple-element.24.f_ref, f32[2,4,4,64,128]{4,3,2,1,0:T(8,128)} %get-tuple-element.25.a_ref, f32[2,2,3,4,64,128]{5,4,3,2,1,0:T(8,128)S(1)} %add_flux.1.part, ...), custom_call_target="tpu_custom_call", output_to_operand_aliasing={{0}: (0, {}), {1}: (1, {})} | custom-call | tf_op jit(solution)/shard_map/add_time/pallas_call | solution.py:369
  (1 shorter events, 0.0 us)
Async XLA Ops:
  3.8 11.4 %collective-permute-start.1 = (f32[2,2,7,64,128]{4,3,2,1,0:T(8,128)}, f32[2,2,7,64,128]{4,3,2,1,0:T(8,128)S(1)}, u32[]{:S(2)}, u32[]{:S(2)}) collective-permute-start(f32[2,2,7,64,128]{4,3,2,1,0:T(8,128)} %get-tuple-element.17), channel_id=1, source_target_pairs={{0,1},{1,0},{2,3},{3,2},{4,5},{5,4},{6,7},{7,6},{8,9},{9,8},{10,11... | collective-permute-start | bytes 2752520 | tf_op jit(solution)/shard_map/ppermute | solution.py:525
  4.5 26.1 %collective-permute-start = (f32[2,2,3,64,128]{4,3,2,1,0:T(8,128)}, f32[2,2,3,64,128]{4,3,2,1,0:T(8,128)S(1)}, u32[]{:S(2)}, u32[]{:S(2)}) collective-permute-start(f32[2,2,3,64,128]{4,3,2,1,0:T(8,128)} %get-tuple-element.16), channel_id=1, source_target_pairs={{1,2},{2,1},{3,4},{4,3},{5,6},{6,5},{7,8},{8,7},{9,10},{10,9},{11,... | collective-permute-start | bytes 1179656 | tf_op jit(solution)/shard_map/ppermute | solution.py:527
  9.9 31.4 %all-to-all-start = ((f32[8,2,6,32,128]{4,3,2,1,0:T(8,128)}), f32[8,2,6,32,128]{4,3,2,1,0:T(8,128)S(1)}, u32[]{:S(2)}, u32[]{:S(2)}) async-start(f32[8,2,6,32,128]{4,3,2,1,0:T(8,128)} %get-tuple-element.15), calls=%async_computation | async-start | bytes 3145728 | tf_op jit(solution)/shard_map/all_to_all | solution.py:530
  15.1 0.9 %copy-start.2 = (f32[2,2,7,64,128]{4,3,2,1,0:T(8,128)}, f32[2,2,7,64,128]{4,3,2,1,0:T(8,128)S(1)}, u32[]{:S(2)}) copy-start(f32[2,2,7,64,128]{4,3,2,1,0:T(8,128)S(1)} %collective-permute-done.1.near_ref) | copy-start | bytes 2752516
  30.6 0.7 %copy-start.3 = (f32[2,2,3,64,128]{4,3,2,1,0:T(8,128)}, f32[2,2,3,64,128]{4,3,2,1,0:T(8,128)S(1)}, u32[]{:S(2)}) copy-start(f32[2,2,3,64,128]{4,3,2,1,0:T(8,128)S(1)} %collective-permute-done.far_ref) | copy-start | bytes 1179652
  35.6 17.4 %collective-permute-start.2 = (f32[2,2,3,64,128]{4,3,2,1,0:T(8,128)}, f32[2,2,3,64,128]{4,3,2,1,0:T(8,128)S(1)}, u32[]{:S(2)}, u32[]{:S(2)}) collective-permute-start(f32[2,2,3,64,128]{4,3,2,1,0:T(8,128)} %get-tuple-element.26), channel_id=1, source_target_pairs={{1,2},{2,1},{3,4},{4,3},{5,6},{6,5},{7,8},{8,7},{9,10},{10,9},{11,... | collective-permute-start | bytes 1179656 | tf_op jit(solution)/shard_map/ppermute | solution.py:538
  42.9 8.0 %copy-start = (f32[2,4,4,64,128]{4,3,2,1,0:T(8,128)S(1)}, f32[2,4,4,64,128]{4,3,2,1,0:T(8,128)}, u32[]{:S(2)}) copy-start(f32[2,4,4,64,128]{4,3,2,1,0:T(8,128)} %get-tuple-element.24.f_ref) | copy-start | bytes 3145732
  42.9 26.2 %all-to-all-start.1 = ((f32[8,2,6,32,128]{4,3,2,1,0:T(8,128)}), f32[8,2,6,32,128]{4,3,2,1,0:T(8,128)S(1)}, u32[]{:S(2)}, u32[]{:S(2)}) async-start(f32[8,2,6,32,128]{4,3,2,1,0:T(8,128)} %bitcast.4), calls=%async_computation.1 | async-start | bytes 3145728 | tf_op jit(solution)/shard_map/all_to_all | solution.py:542
  51.0 1.2 %copy-start.1 = (f32[2,4,4,64,128]{4,3,2,1,0:T(8,128)S(1)}, f32[2,4,4,64,128]{4,3,2,1,0:T(8,128)}, u32[]{:S(2)}) copy-start(f32[2,4,4,64,128]{4,3,2,1,0:T(8,128)} %get-tuple-element.25.a_ref) | copy-start | bytes 3145732

commit v4 on v3

--- a/solution.py
+++ b/solution.py
@@ -243,7 +243,7 @@
     data = pl.ds(TOP, ROWS)
     pair, partial, own = pl.ds(2 * core, 2), pl.ds(1 + core, 1), pl.ds(2 + 2 * core, 2)
     edge, last = 2 + 3 * core, 3 * core
-    reads, parts, writes = [], [], []
+    reads, writes = [], []
     for i in range(insts):
         copies = []
         for n, source in enumerate((flow_ref, adj_ref)):
@@ -252,24 +252,20 @@
             copies.append((source.at[i, 3, pair], w.at[i, 6 + n, own, data, :]))
             copies.append((far_ref.at[i, n], w.at[i, vel, 1 + 5 * core, data, :]))
         reads.append([pltpu.make_async_copy(a, b, sems.at[i, k]) for k, (a, b) in enumerate(copies)])
-        copies = [(a.at[i, :, partial], b.at[i, :, partial]) for a, b in ((flow_out, out_f), (adj_out, out_a))]
-        copies += [(a.at[i], b.at[i, :, 3:5]) for a, b in ((tx_part, tx), (fx_part, fx))]
-        parts.append([pltpu.make_async_copy(a, b, part_sems.at[i, k]) for k, (a, b) in enumerate(copies)])
         copies = [(a.at[i, :, edge], sent.at[i, n]) for n, a in enumerate((tx, fx))]
-        copies += [(a.at[i, :, pair], b.at[i, :, pair]) for a, b in ((out_f, flow_out), (out_a, adj_out))]
+        copies += [(a.at[i, :, last], b.at[i, :, last]) for a, b in ((out_f, flow_out), (out_a, adj_out))]
         writes.append([pltpu.make_async_copy(a, b, out_sems.at[i, k]) for k, (a, b) in enumerate(copies)])
     here = pl.ds(last, 1)
     cells = zip(cells_hbm, (density_ref, mask_ref, labels_ref))
     reads[0] += [pltpu.make_async_copy(a.at[here], b.at[here], cell_sems.at[k]) for k, (a, b) in enumerate(cells)]
     for i in range(insts):
-        for h in reads[i] + parts[i]:
+        for h in reads[i]:
             h.start()
     for i in range(insts):
         clear_edges(w, i, 1 + 3 * core, 3)
     tile_work, y_edges, collect, over = stencil_tools(
         inflow_ref, w, tx, fx, ty, fy, out_f, out_a, density_ref, mask_ref, labels_ref
     )
-    sign = at_end * (1.0 - 2.0 * core.astype(jnp.float32))
 
     def beyond(i, t):
         r = pl.multiple_of(t * TILE, 8)
@@ -278,8 +274,8 @@
         lam = [w[i, 3 + j, edge, here, :] for j in range(3)]
         outer_t, outer_f = outer_cell(u, lam, 0)
         for j in range(3):
-            tx[i, j, 1 + 5 * core, pl.ds(r, TILE), :] = sign * outer_t[j]
-            fx[i, j, 1 + 5 * core, pl.ds(r, TILE), :] = sign * outer_f[j]
+            out_f[i, j, last, pl.ds(r, TILE), :] += at_end * outer_t[j]
+            out_a[i, j, last, pl.ds(r, TILE), :] += at_end * outer_f[j]
 
     for i in range(insts):
         for h in reads[i]:
@@ -289,10 +285,7 @@
             h.start()
         y_edges(i, last)
         over(edge, 1, lambda p, t: beyond(i, t))
-        for h in parts[i]:
-            h.wait()
-        over(edge, 1, lambda p, t: collect(i, p, t, True, True))
-        over(3 + core, 1, lambda p, t: collect(i, p, t, True, False))
+        over(edge, 1, lambda p, t: collect(i, p, t, False, True))
         for h in writes[i][2:]:
             h.start()
     for group in writes:
@@ -324,26 +317,29 @@
     )(flow_part, adj_part)
 
 
-def flux_kernel(core_ref, part, flux, total):
+def flux_kernel(core_ref, part, flux, leaving, tx_part, fx_part, total):
     core = core_ref[0]
     sign = 1.0 - 2.0 * core.astype(jnp.float32)
     for i in range(part.shape[0]):
         for n in range(2):
             total[i, n] = part[i, n]
-            total[i, n, :, 3 * core] = part[i, n, :, 3 * core] + sign * flux[i, n]
-
-
-def add_flux(core, part, flux):
+            flux_x = (tx_part, fx_part)[n]
+            near, next_one = flux_x[i, :, core], flux_x[i, :, 1 - core]
+            total[i, n, :, 3 * core] = part[i, n, :, 3 * core] - sign * (near - flux[i, n])
+            total[i, n, :, 1 + core] = part[i, n, :, 1 + core] - sign * (next_one - leaving[i, n])
+
+
+def add_flux(core, part, *fluxes):
     whole = pl.BlockSpec(memory_space=pltpu.VMEM)
     return pl.pallas_call(
         flux_kernel,
         out_shape=jax.ShapeDtypeStruct(part.shape, jnp.float32),
-        in_specs=[pl.BlockSpec(memory_space=pltpu.SMEM)] + [whole] * 2,
+        in_specs=[pl.BlockSpec(memory_space=pltpu.SMEM)] + [whole] * (1 + len(fluxes)),
         out_specs=whole,
         compiler_params=pltpu.CompilerParams(vmem_limit_bytes=ADD_LIMIT),
         cost_estimate=pl.CostEstimate(flops=LATE_COST, bytes_accessed=8_000_000, transcendentals=0),
         name="add_flux",
-    )(core, part, flux)
+    )(core, part, *fluxes)
 
 
 def add_kernel(f_ref, a_ref, part, times, out_f, out_a, total, sems):
@@ -534,13 +530,14 @@
         early_kernel, "early", EARLY_COST, [flow.shape] * 2 + [edge] * 2, core, scalars, flow, adj, [near], cells
     )
     shapes = [flow.shape] * 2 + [(insts, 2, 3, ROWS, LANES)]
-    *parts, flux = stencil(late_kernel, "late", LATE_COST, shapes, core, scalars, flow, adj, [far], cells, *parts)
-    flux = lax.ppermute(flux, "space", across)
+    edges = parts[2:]
+    *parts, leaving = stencil(late_kernel, "late", LATE_COST, shapes, core, scalars, flow, adj, [far], cells, *parts)
+    flux = lax.ppermute(leaving, "space", across)
     gathered, *parts = lax.optimization_barrier((gathered, *parts))
     by_time = (NT,) + blocks.shape[2:]
     derived = time_derivative(gathered.reshape(by_time), blocks.reshape(by_time))
     time_part = lax.all_to_all(derived.reshape(blocks.shape), "tm", 0, 0, tiled=True)
-    return add_time(*parts, add_flux(core, load_parts(*parts), flux), time_part)
+    return add_time(*parts, add_flux(core, load_parts(*parts), flux, leaving, *edges), time_part)
 
 
 def solution(mesh):

time: 70.8 us -> 72 us (1.017)
  starting transfers between devices: 23.5 us -> 27.3 us
  waiting for transfers between devices: 24.3 us -> 21.5 us
    all_to_all x1, starting transfers between devices: 8.01 us -> 11.9 us  [on_device(): lax.all_to_all(derived.reshape(blocks.shape), 'tm', 0, 0, tiled=True)]
    all_to_all x1, waiting for transfers between devices: 16 us -> 12.8 us  [on_device(): lax.all_to_all(derived.reshape(blocks.shape), 'tm', 0, 0, tiled=True)]
    unnamed x8 -> x14, local copies, waits for them, and re-layouts: 2.89 us -> 3.34 us
  transfers between devices with their start and end apart: 5 -> 5, of which waited for: 3 -> 3; matrix products, arithmetic and copies ran while one was open for 1% -> 1% of each run, Pallas kernels for 20% -> 19%
where the time goes in v4:
time: 72 us; the launch traced here: 71.6 us
  starting transfers between devices  27.3 us (38%)
  waiting for transfers between devices  21.5 us (30%)
  Pallas kernels  18 us (25%)
  local copies, waits for them, and re-layouts  3.34 us (5%)
  between operations  0.74 us (1%)
    all_to_all x1, waiting for transfers between devices, on_device(): lax.all_to_all(derived.reshape(blocks.shape), 'tm', 0, 0, tiled=True)  12.8 us
    all_to_all x1, starting transfers between devices, on_device(): lax.all_to_all(derived.reshape(blocks.shape), 'tm', 0, 0, tiled=True)  11.9 us
    pallas_call x2, Pallas kernels, stencil(): pl.pallas_call(kernel, out_shape=[jax.ShapeDtypeStruct(s, jnp.float32) fo...  11 us
    ppermute x1, waiting for transfers between devices, on_device(): far = lax.ppermute(far, 'space', across)  7.55 us
    ppermute x1, starting transfers between devices, on_device(): far = lax.ppermute(far, 'space', across)  5.4 us
    ppermute x1, starting transfers between devices, on_device(): flux = lax.ppermute(leaving, 'space', across)  4.79 us
    all_to_all x1, starting transfers between devices, on_device(): gathered = lax.all_to_all(blocks, 'tm', 0, 0, tiled=True)  4.49 us
    unnamed x14, local copies, waits for them, and re-layouts  3.34 us
  transfers between devices with their start and end apart: 5, of which 3 were waited for; matrix products, arithmetic and copies ran while one was open for 1% of the time, Pallas kernels for 19%

profile of v4, /device:TPU:17, one launch (start us, length us, event | category | flops | bytes accessed | tf_op | source)
XLA Modules:
  0.0 71.6 jit_solution(8415878459272544955)
XLA Ops:
  0.6 3.1 %pack.1 = (f32[8,2,6,32,128]{4,3,2,1,0:T(8,128)}, f32[2,2,7,64,128]{4,3,2,1,0:T(8,128)}, f32[2,2,3,64,128]{4,3,2,1,0:T(8,128)}) custom-call(s32[1]{0:T(128)} %bitcast.core_ref, f32[2,4,4,64,128]{4,3,2,1,0:T(8,128)} %flow_ref.5, f32[2,4,4,64,128]{4,3,2,1,0:T(8,128)} %adj_ref.5), custom_call_target="tpu_custom_call" | custom-call | tf_op jit(solution)/shard_map/pack/pallas_call | solution.py:494
  3.8 0.8 %collective-permute-start.1 = (f32[2,2,7,64,128]{4,3,2,1,0:T(8,128)}, f32[2,2,7,64,128]{4,3,2,1,0:T(8,128)S(1)}, u32[]{:S(2)}, u32[]{:S(2)}) collective-permute-start(f32[2,2,7,64,128]{4,3,2,1,0:T(8,128)} %get-tuple-element.17), channel_id=1, source_target_pairs={{0,1},{1,0},{2,3},{3,2},{4,5},{5,4},{6,7},{7,6},{8,9},{9,8},{10,11... | collective-permute-start | bytes 2752520 | tf_op jit(solution)/shard_map/ppermute | solution.py:521
  4.5 5.4 %collective-permute-start = (f32[2,2,3,64,128]{4,3,2,1,0:T(8,128)}, f32[2,2,3,64,128]{4,3,2,1,0:T(8,128)S(1)}, u32[]{:S(2)}, u32[]{:S(2)}) collective-permute-start(f32[2,2,3,64,128]{4,3,2,1,0:T(8,128)} %get-tuple-element.16), channel_id=1, source_target_pairs={{1,2},{2,1},{3,4},{4,3},{5,6},{6,5},{7,8},{8,7},{9,10},{10,9},{11,... | collective-permute-start | bytes 1179656 | tf_op jit(solution)/shard_map/ppermute | solution.py:523
  9.9 4.5 %all-to-all-start = ((f32[8,2,6,32,128]{4,3,2,1,0:T(8,128)}), f32[8,2,6,32,128]{4,3,2,1,0:T(8,128)S(1)}, u32[]{:S(2)}, u32[]{:S(2)}) async-start(f32[8,2,6,32,128]{4,3,2,1,0:T(8,128)} %get-tuple-element.15), calls=%async_computation | async-start | bytes 3145728 | tf_op jit(solution)/shard_map/all_to_all | solution.py:526
  14.5 0.6 pad_maximum_fusion.inflow_ref
  15.1 0.0 collective-permute-done.1.near_ref
  15.1 0.0 copy-start.5
  15.1 0.9 %copy-done.5 = f32[2,2,7,64,128]{4,3,2,1,0:T(8,128)} copy-done((f32[2,2,7,64,128]{4,3,2,1,0:T(8,128)}, f32[2,2,7,64,128]{4,3,2,1,0:T(8,128)S(1)}, u32[]{:S(2)}) %copy-start.5) | copy-done | bytes 917528
  16.0 7.0 %early.1 = (f32[2,4,4,64,128]{4,3,2,1,0:T(8,128)}, f32[2,4,4,64,128]{4,3,2,1,0:T(8,128)}, f32[2,3,2,64,128]{4,3,2,1,0:T(8,128)}, f32[2,3,2,64,128]{4,3,2,1,0:T(8,128)}) custom-call(s32[1]{0:T(128)} %bitcast.core_ref, f32[3]{0:T(128)} %pad_maximum_fusion.inflow_ref, f32[2,4,4,64,128]{4,3,2,1,0:T(8,128)} %flow_ref.5, f32[2,4,4,64,128]{4,3,2,1,0:T(8,128)} %adj_ref.5, ...), custom_call_target="tpu_custom_call" | custom-call | flops 20000000000 | bytes 8000000 | tf_op jit(solution)/shard_map/early/pallas_call | solution.py:383
  23.1 7.5 %collective-permute-done.far_ref = f32[2,2,3,64,128]{4,3,2,1,0:T(8,128)S(1)} collective-permute-done((f32[2,2,3,64,128]{4,3,2,1,0:T(8,128)}, f32[2,2,3,64,128]{4,3,2,1,0:T(8,128)S(1)}, u32[]{:S(2)}, u32[]{:S(2)}) %collective-permute-start) | collective-permute-done | bytes 393248 | tf_op jit(solution)/shard_map/ppermute | solution.py:523
  30.6 0.0 copy-start.6
  30.6 0.8 %copy-done.6 = f32[2,2,3,64,128]{4,3,2,1,0:T(8,128)} copy-done((f32[2,2,3,64,128]{4,3,2,1,0:T(8,128)}, f32[2,2,3,64,128]{4,3,2,1,0:T(8,128)S(1)}, u32[]{:S(2)}) %copy-start.6) | copy-done | bytes 393240
  31.4 4.0 %late.1 = (f32[2,4,4,64,128]{4,3,2,1,0:T(8,128)}, f32[2,4,4,64,128]{4,3,2,1,0:T(8,128)}, f32[2,2,3,64,128]{4,3,2,1,0:T(8,128)}) custom-call(s32[1]{0:T(128)} %bitcast.core_ref, f32[3]{0:T(128)} %pad_maximum_fusion.inflow_ref, f32[2,4,4,64,128]{4,3,2,1,0:T(8,128)} %flow_ref.5, ...), custom_call_target="tpu_custom_call", output_to_operand_aliasing={{0}: (8, {}), {1}: (9, {})} | custom-call | flops 40000000000 | bytes 8000000 | tf_op jit(solution)/shard_map/late/pallas_call | solution.py:383
  35.3 4.8 %collective-permute-start.2 = (f32[2,2,3,64,128]{4,3,2,1,0:T(8,128)}, f32[2,2,3,64,128]{4,3,2,1,0:T(8,128)S(1)}, u32[]{:S(2)}, u32[]{:S(2)}) collective-permute-start(f32[2,2,3,64,128]{4,3,2,1,0:T(8,128)} %get-tuple-element.26.leaving), channel_id=1, source_target_pairs={{1,2},{2,1},{3,4},{4,3},{5,6},{6,5},{7,8},{8,7},{9,10},{10,9},{11,... | collective-permute-start | bytes 1179656 | tf_op jit(solution)/shard_map/ppermute | solution.py:535
  40.1 1.2 %all-to-all-done = f32[8,2,6,32,128]{4,3,2,1,0:T(8,128)S(1)} async-done(((f32[8,2,6,32,128]{4,3,2,1,0:T(8,128)}), f32[8,2,6,32,128]{4,3,2,1,0:T(8,128)S(1)}, u32[]{:S(2)}, u32[]{:S(2)}) %all-to-all-start) | async-done | bytes 1572896 | tf_op jit(solution)/shard_map/all_to_all | solution.py:526
  41.3 1.6 %time_derivative.1 = f32[16,6,32,128]{3,2,1,0:T(8,128)} custom-call(f32[16,6,32,128]{3,2,1,0:T(8,128)S(1)} %bitcast.5, f32[16,6,32,128]{3,2,1,0:T(8,128)} %bitcast.3.sent_hbm), custom_call_target="tpu_custom_call", output_to_operand_aliasing={{}: (1, {})} | custom-call | flops 12000000 | bytes 3200000 | tf_op jit(solution)/shard_map/time_derivative/pallas_call | solution.py:430
  42.9 0.0 copy-start
  42.9 11.9 %all-to-all-start.1 = ((f32[8,2,6,32,128]{4,3,2,1,0:T(8,128)}), f32[8,2,6,32,128]{4,3,2,1,0:T(8,128)S(1)}, u32[]{:S(2)}, u32[]{:S(2)}) async-start(f32[8,2,6,32,128]{4,3,2,1,0:T(8,128)} %bitcast.4), calls=%async_computation.1 | async-start | bytes 3145728 | tf_op jit(solution)/shard_map/all_to_all | solution.py:539
  54.8 0.0 copy-done
  54.8 0.0 copy-start.1
  54.8 1.2 %copy-done.1 = f32[2,4,4,64,128]{4,3,2,1,0:T(8,128)S(1)} copy-done((f32[2,4,4,64,128]{4,3,2,1,0:T(8,128)S(1)}, f32[2,4,4,64,128]{4,3,2,1,0:T(8,128)}, u32[]{:S(2)}) %copy-start.1) | copy-done | bytes 1048600
  56.1 0.0 copy-start.2
  56.1 0.0 copy-start.3
  56.1 0.0 copy-start.4
  56.1 0.8 %load_parts.1.part = f32[2,2,3,4,64,128]{5,4,3,2,1,0:T(8,128)S(1)} custom-call(f32[2,4,4,64,128]{4,3,2,1,0:T(8,128)S(1)} %copy-done, f32[2,4,4,64,128]{4,3,2,1,0:T(8,128)S(1)} %copy-done.1), custom_call_target="tpu_custom_call" | custom-call | tf_op jit(solution)/shard_map/load_parts/pallas_call | solution.py:309
  56.9 0.0 collective-permute-done.2.flux
  56.9 0.2 copy-done.2
  57.1 0.1 copy-done.3
  57.2 0.1 copy-done.4
  57.3 0.2 add_flux.1.part
  57.5 12.8 %all-to-all-done.1.times = f32[8,2,6,32,128]{4,3,2,1,0:T(8,128)S(1)} async-done(((f32[8,2,6,32,128]{4,3,2,1,0:T(8,128)}), f32[8,2,6,32,128]{4,3,2,1,0:T(8,128)S(1)}, u32[]{:S(2)}, u32[]{:S(2)}) %all-to-all-start.1) | async-done | bytes 1572896 | tf_op jit(solution)/shard_map/all_to_all | solution.py:539
  70.3 1.2 %add_time.1 = (f32[2,4,4,64,128]{4,3,2,1,0:T(8,128)}, f32[2,4,4,64,128]{4,3,2,1,0:T(8,128)}) custom-call(f32[2,4,4,64,128]{4,3,2,1,0:T(8,128)} %get-tuple-element.24.f_ref, f32[2,4,4,64,128]{4,3,2,1,0:T(8,128)} %get-tuple-element.25.a_ref, f32[2,2,3,4,64,128]{5,4,3,2,1,0:T(8,128)S(1)} %add_flux.1.part, ...), custom_call_target="tpu_custom_call", output_to_operand_aliasing={{0}: (0, {}), {1}: (1, {})} | custom-call | tf_op jit(solution)/shard_map/add_time/pallas_call | solution.py:365
  (1 shorter events, 0.0 us)
Async XLA Ops:
  3.8 11.3 %collective-permute-start.1 = (f32[2,2,7,64,128]{4,3,2,1,0:T(8,128)}, f32[2,2,7,64,128]{4,3,2,1,0:T(8,128)S(1)}, u32[]{:S(2)}, u32[]{:S(2)}) collective-permute-start(f32[2,2,7,64,128]{4,3,2,1,0:T(8,128)} %get-tuple-element.17), channel_id=1, source_target_pairs={{0,1},{1,0},{2,3},{3,2},{4,5},{5,4},{6,7},{7,6},{8,9},{9,8},{10,11... | collective-permute-start | bytes 2752520 | tf_op jit(solution)/shard_map/ppermute | solution.py:521
  4.5 26.1 %collective-permute-start = (f32[2,2,3,64,128]{4,3,2,1,0:T(8,128)}, f32[2,2,3,64,128]{4,3,2,1,0:T(8,128)S(1)}, u32[]{:S(2)}, u32[]{:S(2)}) collective-permute-start(f32[2,2,3,64,128]{4,3,2,1,0:T(8,128)} %get-tuple-element.16), channel_id=1, source_target_pairs={{1,2},{2,1},{3,4},{4,3},{5,6},{6,5},{7,8},{8,7},{9,10},{10,9},{11,... | collective-permute-start | bytes 1179656 | tf_op jit(solution)/shard_map/ppermute | solution.py:523
  9.9 31.4 %all-to-all-start = ((f32[8,2,6,32,128]{4,3,2,1,0:T(8,128)}), f32[8,2,6,32,128]{4,3,2,1,0:T(8,128)S(1)}, u32[]{:S(2)}, u32[]{:S(2)}) async-start(f32[8,2,6,32,128]{4,3,2,1,0:T(8,128)} %get-tuple-element.15), calls=%async_computation | async-start | bytes 3145728 | tf_op jit(solution)/shard_map/all_to_all | solution.py:526
  15.1 0.9 %copy-start.5 = (f32[2,2,7,64,128]{4,3,2,1,0:T(8,128)}, f32[2,2,7,64,128]{4,3,2,1,0:T(8,128)S(1)}, u32[]{:S(2)}) copy-start(f32[2,2,7,64,128]{4,3,2,1,0:T(8,128)S(1)} %collective-permute-done.1.near_ref) | copy-start | bytes 2752516
  30.6 0.8 %copy-start.6 = (f32[2,2,3,64,128]{4,3,2,1,0:T(8,128)}, f32[2,2,3,64,128]{4,3,2,1,0:T(8,128)S(1)}, u32[]{:S(2)}) copy-start(f32[2,2,3,64,128]{4,3,2,1,0:T(8,128)S(1)} %collective-permute-done.far_ref) | copy-start | bytes 1179652
  35.3 21.5 %collective-permute-start.2 = (f32[2,2,3,64,128]{4,3,2,1,0:T(8,128)}, f32[2,2,3,64,128]{4,3,2,1,0:T(8,128)S(1)}, u32[]{:S(2)}, u32[]{:S(2)}) collective-permute-start(f32[2,2,3,64,128]{4,3,2,1,0:T(8,128)} %get-tuple-element.26.leaving), channel_id=1, source_target_pairs={{1,2},{2,1},{3,4},{4,3},{5,6},{6,5},{7,8},{8,7},{9,10},{10,9},{11,... | collective-permute-start | bytes 1179656 | tf_op jit(solution)/shard_map/ppermute | solution.py:535
  42.9 11.9 %copy-start = (f32[2,4,4,64,128]{4,3,2,1,0:T(8,128)S(1)}, f32[2,4,4,64,128]{4,3,2,1,0:T(8,128)}, u32[]{:S(2)}) copy-start(f32[2,4,4,64,128]{4,3,2,1,0:T(8,128)} %get-tuple-element.24.f_ref) | copy-start | bytes 3145732
  42.9 27.4 %all-to-all-start.1 = ((f32[8,2,6,32,128]{4,3,2,1,0:T(8,128)}), f32[8,2,6,32,128]{4,3,2,1,0:T(8,128)S(1)}, u32[]{:S(2)}, u32[]{:S(2)}) async-start(f32[8,2,6,32,128]{4,3,2,1,0:T(8,128)} %bitcast.4), calls=%async_computation.1 | async-start | bytes 3145728 | tf_op jit(solution)/shard_map/all_to_all | solution.py:539
  54.8 1.2 %copy-start.1 = (f32[2,4,4,64,128]{4,3,2,1,0:T(8,128)S(1)}, f32[2,4,4,64,128]{4,3,2,1,0:T(8,128)}, u32[]{:S(2)}) copy-start(f32[2,4,4,64,128]{4,3,2,1,0:T(8,128)} %get-tuple-element.25.a_ref) | copy-start | bytes 3145732
  56.1 1.0 %copy-start.2 = (f32[2,2,3,64,128]{4,3,2,1,0:T(8,128)S(1)}, f32[2,2,3,64,128]{4,3,2,1,0:T(8,128)}, u32[]{:S(2)}) copy-start(f32[2,2,3,64,128]{4,3,2,1,0:T(8,128)} %get-tuple-element.26.leaving) | copy-start | bytes 1179652
  56.1 1.1 %copy-start.3 = (f32[2,3,2,64,128]{4,3,2,1,0:T(8,128)S(1)}, f32[2,3,2,64,128]{4,3,2,1,0:T(8,128)}, u32[]{:S(2)}) copy-start(f32[2,3,2,64,128]{4,3,2,1,0:T(8,128)} %get-tuple-element.20.refs_5_.tx_part) | copy-start | bytes 1179652
  56.1 1.2 %copy-start.4 = (f32[2,3,2,64,128]{4,3,2,1,0:T(8,128)S(1)}, f32[2,3,2,64,128]{4,3,2,1,0:T(8,128)}, u32[]{:S(2)}) copy-start(f32[2,3,2,64,128]{4,3,2,1,0:T(8,128)} %get-tuple-element.21.refs_6_.fx_part) | copy-start | bytes 1179652

commit v5 on v3

--- a/solution.py
+++ b/solution.py
@@ -22,8 +22,8 @@
 LANES = 128
 TOP = 8
 PADDED = ROWS + 2 * TOP
-TILE = 32
-UNROLL = 2
+TILE = 64
+UNROLL = 1
 VMEM_LIMIT = 56 << 20
 EARLY_COST = 20_000_000_000
 LATE_COST = 40_000_000_000

time: 70.8 us -> 72 us (1.017)
  starting transfers between devices: 23.5 us -> 27.6 us
  waiting for transfers between devices: 24.3 us -> 21.6 us
    all_to_all x1, starting transfers between devices: 8.01 us -> 12.2 us  [on_device(): lax.all_to_all(derived.reshape(blocks.shape), 'tm', 0, 0, tiled=True)]
    all_to_all x1, waiting for transfers between devices: 16 us -> 13 us  [on_device(): lax.all_to_all(derived.reshape(blocks.shape), 'tm', 0, 0, tiled=True)]
  transfers between devices with their start and end apart: 5 -> 5, of which waited for: 3 -> 3; matrix products, arithmetic and copies ran while one was open for 1% -> 1% of each run, Pallas kernels for 20% -> 19%
where the time goes in v5:
time: 72 us; the launch traced here: 71.6 us
  starting transfers between devices  27.6 us (38%)
  waiting for transfers between devices  21.6 us (30%)
  Pallas kernels  18 us (25%)
  local copies, waits for them, and re-layouts  2.89 us (4%)
  between operations  0.74 us (1%)
    all_to_all x1, waiting for transfers between devices, on_device(): lax.all_to_all(derived.reshape(blocks.shape), 'tm', 0, 0, tiled=True)  13 us
    all_to_all x1, starting transfers between devices, on_device(): lax.all_to_all(derived.reshape(blocks.shape), 'tm', 0, 0, tiled=True)  12.2 us
    pallas_call x2, Pallas kernels, stencil(): pl.pallas_call(kernel, out_shape=[jax.ShapeDtypeStruct(s, jnp.float32) fo...  11.1 us
    ppermute x1, waiting for transfers between devices, on_device(): far = lax.ppermute(far, 'space', across)  7.71 us
    ppermute x1, starting transfers between devices, on_device(): far = lax.ppermute(far, 'space', across)  5.4 us
    ppermute x1, starting transfers between devices, on_device(): flux = lax.ppermute(flux, 'space', across)  4.81 us
    all_to_all x1, starting transfers between devices, on_device(): gathered = lax.all_to_all(blocks, 'tm', 0, 0, tiled=True)  4.49 us
    pallas_call x1, Pallas kernels, pack(): pl.pallas_call(pack_kernel, out_shape=[jax.ShapeDtypeStruct(s, jnp.float3...  3.12 us
  transfers between devices with their start and end apart: 5, of which 3 were waited for; matrix products, arithmetic and copies ran while one was open for 1% of the time, Pallas kernels for 19%

profile of v5, /device:TPU:17, one launch (start us, length us, event | category | flops | bytes accessed | tf_op | source)
XLA Modules:
  0.0 71.6 jit_solution(16065444575308997236)
XLA Ops:
  0.6 3.1 %pack.1 = (f32[8,2,6,32,128]{4,3,2,1,0:T(8,128)}, f32[2,2,7,64,128]{4,3,2,1,0:T(8,128)}, f32[2,2,3,64,128]{4,3,2,1,0:T(8,128)}) custom-call(s32[1]{0:T(128)} %bitcast.core_ref, f32[2,4,4,64,128]{4,3,2,1,0:T(8,128)} %flow_ref.5, f32[2,4,4,64,128]{4,3,2,1,0:T(8,128)} %adj_ref.5), custom_call_target="tpu_custom_call" | custom-call | tf_op jit(solution)/shard_map/pack/pallas_call | solution.py:498
  3.8 0.8 %collective-permute-start.1 = (f32[2,2,7,64,128]{4,3,2,1,0:T(8,128)}, f32[2,2,7,64,128]{4,3,2,1,0:T(8,128)S(1)}, u32[]{:S(2)}, u32[]{:S(2)}) collective-permute-start(f32[2,2,7,64,128]{4,3,2,1,0:T(8,128)} %get-tuple-element.17), channel_id=1, source_target_pairs={{0,1},{1,0},{2,3},{3,2},{4,5},{5,4},{6,7},{7,6},{8,9},{9,8},{10,11... | collective-permute-start | bytes 2752520 | tf_op jit(solution)/shard_map/ppermute | solution.py:525
  4.5 5.4 %collective-permute-start = (f32[2,2,3,64,128]{4,3,2,1,0:T(8,128)}, f32[2,2,3,64,128]{4,3,2,1,0:T(8,128)S(1)}, u32[]{:S(2)}, u32[]{:S(2)}) collective-permute-start(f32[2,2,3,64,128]{4,3,2,1,0:T(8,128)} %get-tuple-element.16), channel_id=1, source_target_pairs={{1,2},{2,1},{3,4},{4,3},{5,6},{6,5},{7,8},{8,7},{9,10},{10,9},{11,... | collective-permute-start | bytes 1179656 | tf_op jit(solution)/shard_map/ppermute | solution.py:527
  9.9 4.5 %all-to-all-start = ((f32[8,2,6,32,128]{4,3,2,1,0:T(8,128)}), f32[8,2,6,32,128]{4,3,2,1,0:T(8,128)S(1)}, u32[]{:S(2)}, u32[]{:S(2)}) async-start(f32[8,2,6,32,128]{4,3,2,1,0:T(8,128)} %get-tuple-element.15), calls=%async_computation | async-start | bytes 3145728 | tf_op jit(solution)/shard_map/all_to_all | solution.py:530
  14.5 0.7 pad_maximum_fusion.inflow_ref
  15.1 0.0 collective-permute-done.1.near_ref
  15.1 0.0 copy-start.2
  15.1 0.9 %copy-done.2 = f32[2,2,7,64,128]{4,3,2,1,0:T(8,128)} copy-done((f32[2,2,7,64,128]{4,3,2,1,0:T(8,128)}, f32[2,2,7,64,128]{4,3,2,1,0:T(8,128)S(1)}, u32[]{:S(2)}) %copy-start.2) | copy-done | bytes 917528
  16.1 6.8 %early.1 = (f32[2,4,4,64,128]{4,3,2,1,0:T(8,128)}, f32[2,4,4,64,128]{4,3,2,1,0:T(8,128)}, f32[2,3,2,64,128]{4,3,2,1,0:T(8,128)}, f32[2,3,2,64,128]{4,3,2,1,0:T(8,128)}) custom-call(s32[1]{0:T(128)} %bitcast.core_ref, f32[3]{0:T(128)} %pad_maximum_fusion.inflow_ref, f32[2,4,4,64,128]{4,3,2,1,0:T(8,128)} %flow_ref.5, f32[2,4,4,64,128]{4,3,2,1,0:T(8,128)} %adj_ref.5, ...), custom_call_target="tpu_custom_call" | custom-call | flops 20000000000 | bytes 8000000 | tf_op jit(solution)/shard_map/early/pallas_call | solution.py:387
  22.9 7.7 %collective-permute-done.far_ref = f32[2,2,3,64,128]{4,3,2,1,0:T(8,128)S(1)} collective-permute-done((f32[2,2,3,64,128]{4,3,2,1,0:T(8,128)}, f32[2,2,3,64,128]{4,3,2,1,0:T(8,128)S(1)}, u32[]{:S(2)}, u32[]{:S(2)}) %collective-permute-start) | collective-permute-done | bytes 393248 | tf_op jit(solution)/shard_map/ppermute | solution.py:527
  30.6 0.0 copy-start.3
  30.6 0.7 %copy-done.3 = f32[2,2,3,64,128]{4,3,2,1,0:T(8,128)} copy-done((f32[2,2,3,64,128]{4,3,2,1,0:T(8,128)}, f32[2,2,3,64,128]{4,3,2,1,0:T(8,128)S(1)}, u32[]{:S(2)}) %copy-start.3) | copy-done | bytes 393240
  31.3 4.3 %late.1 = (f32[2,4,4,64,128]{4,3,2,1,0:T(8,128)}, f32[2,4,4,64,128]{4,3,2,1,0:T(8,128)}, f32[2,2,3,64,128]{4,3,2,1,0:T(8,128)}) custom-call(s32[1]{0:T(128)} %bitcast.core_ref, f32[3]{0:T(128)} %pad_maximum_fusion.inflow_ref, f32[2,4,4,64,128]{4,3,2,1,0:T(8,128)} %flow_ref.5, ...), custom_call_target="tpu_custom_call", output_to_operand_aliasing={{0}: (8, {}), {1}: (9, {})} | custom-call | flops 40000000000 | bytes 8000000 | tf_op jit(solution)/shard_map/late/pallas_call | solution.py:387
  35.6 4.8 %collective-permute-start.2 = (f32[2,2,3,64,128]{4,3,2,1,0:T(8,128)}, f32[2,2,3,64,128]{4,3,2,1,0:T(8,128)S(1)}, u32[]{:S(2)}, u32[]{:S(2)}) collective-permute-start(f32[2,2,3,64,128]{4,3,2,1,0:T(8,128)} %get-tuple-element.26), channel_id=1, source_target_pairs={{1,2},{2,1},{3,4},{4,3},{5,6},{6,5},{7,8},{8,7},{9,10},{10,9},{11,... | collective-permute-start | bytes 1179656 | tf_op jit(solution)/shard_map/ppermute | solution.py:538
  40.4 0.9 %all-to-all-done = f32[8,2,6,32,128]{4,3,2,1,0:T(8,128)S(1)} async-done(((f32[8,2,6,32,128]{4,3,2,1,0:T(8,128)}), f32[8,2,6,32,128]{4,3,2,1,0:T(8,128)S(1)}, u32[]{:S(2)}, u32[]{:S(2)}) %all-to-all-start) | async-done | bytes 1572896 | tf_op jit(solution)/shard_map/all_to_all | solution.py:530
  41.3 1.6 %time_derivative.1 = f32[16,6,32,128]{3,2,1,0:T(8,128)} custom-call(f32[16,6,32,128]{3,2,1,0:T(8,128)S(1)} %bitcast.5, f32[16,6,32,128]{3,2,1,0:T(8,128)} %bitcast.3.sent_hbm), custom_call_target="tpu_custom_call", output_to_operand_aliasing={{}: (1, {})} | custom-call | flops 12000000 | bytes 3200000 | tf_op jit(solution)/shard_map/time_derivative/pallas_call | solution.py:434
  42.9 0.0 copy-start
  42.9 12.2 %all-to-all-start.1 = ((f32[8,2,6,32,128]{4,3,2,1,0:T(8,128)}), f32[8,2,6,32,128]{4,3,2,1,0:T(8,128)S(1)}, u32[]{:S(2)}, u32[]{:S(2)}) async-start(f32[8,2,6,32,128]{4,3,2,1,0:T(8,128)} %bitcast.4), calls=%async_computation.1 | async-start | bytes 3145728 | tf_op jit(solution)/shard_map/all_to_all | solution.py:542
  55.1 0.0 copy-done
  55.1 0.0 copy-start.1
  55.1 1.2 %copy-done.1 = f32[2,4,4,64,128]{4,3,2,1,0:T(8,128)S(1)} copy-done((f32[2,4,4,64,128]{4,3,2,1,0:T(8,128)S(1)}, f32[2,4,4,64,128]{4,3,2,1,0:T(8,128)}, u32[]{:S(2)}) %copy-start.1) | copy-done | bytes 1048600
  56.3 0.8 %load_parts.1.part = f32[2,2,3,4,64,128]{5,4,3,2,1,0:T(8,128)S(1)} custom-call(f32[2,4,4,64,128]{4,3,2,1,0:T(8,128)S(1)} %copy-done, f32[2,4,4,64,128]{4,3,2,1,0:T(8,128)S(1)} %copy-done.1), custom_call_target="tpu_custom_call" | custom-call | tf_op jit(solution)/shard_map/load_parts/pallas_call | solution.py:316
  57.1 0.0 collective-permute-done.2.flux
  57.1 0.1 add_flux.1.part
  57.3 13.0 %all-to-all-done.1.times = f32[8,2,6,32,128]{4,3,2,1,0:T(8,128)S(1)} async-done(((f32[8,2,6,32,128]{4,3,2,1,0:T(8,128)}), f32[8,2,6,32,128]{4,3,2,1,0:T(8,128)S(1)}, u32[]{:S(2)}, u32[]{:S(2)}) %all-to-all-start.1) | async-done | bytes 1572896 | tf_op jit(solution)/shard_map/all_to_all | solution.py:542
  70.3 1.2 %add_time.1 = (f32[2,4,4,64,128]{4,3,2,1,0:T(8,128)}, f32[2,4,4,64,128]{4,3,2,1,0:T(8,128)}) custom-call(f32[2,4,4,64,128]{4,3,2,1,0:T(8,128)} %get-tuple-element.24.f_ref, f32[2,4,4,64,128]{4,3,2,1,0:T(8,128)} %get-tuple-element.25.a_ref, f32[2,2,3,4,64,128]{5,4,3,2,1,0:T(8,128)S(1)} %add_flux.1.part, ...), custom_call_target="tpu_custom_call", output_to_operand_aliasing={{0}: (0, {}), {1}: (1, {})} | custom-call | tf_op jit(solution)/shard_map/add_time/pallas_call | solution.py:369
  (1 shorter events, 0.0 us)
Async XLA Ops:
  3.8 11.4 %collective-permute-start.1 = (f32[2,2,7,64,128]{4,3,2,1,0:T(8,128)}, f32[2,2,7,64,128]{4,3,2,1,0:T(8,128)S(1)}, u32[]{:S(2)}, u32[]{:S(2)}) collective-permute-start(f32[2,2,7,64,128]{4,3,2,1,0:T(8,128)} %get-tuple-element.17), channel_id=1, source_target_pairs={{0,1},{1,0},{2,3},{3,2},{4,5},{5,4},{6,7},{7,6},{8,9},{9,8},{10,11... | collective-permute-start | bytes 2752520 | tf_op jit(solution)/shard_map/ppermute | solution.py:525
  4.5 26.1 %collective-permute-start = (f32[2,2,3,64,128]{4,3,2,1,0:T(8,128)}, f32[2,2,3,64,128]{4,3,2,1,0:T(8,128)S(1)}, u32[]{:S(2)}, u32[]{:S(2)}) collective-permute-start(f32[2,2,3,64,128]{4,3,2,1,0:T(8,128)} %get-tuple-element.16), channel_id=1, source_target_pairs={{1,2},{2,1},{3,4},{4,3},{5,6},{6,5},{7,8},{8,7},{9,10},{10,9},{11,... | collective-permute-start | bytes 1179656 | tf_op jit(solution)/shard_map/ppermute | solution.py:527
  9.9 31.4 %all-to-all-start = ((f32[8,2,6,32,128]{4,3,2,1,0:T(8,128)}), f32[8,2,6,32,128]{4,3,2,1,0:T(8,128)S(1)}, u32[]{:S(2)}, u32[]{:S(2)}) async-start(f32[8,2,6,32,128]{4,3,2,1,0:T(8,128)} %get-tuple-element.15), calls=%async_computation | async-start | bytes 3145728 | tf_op jit(solution)/shard_map/all_to_all | solution.py:530
  15.1 0.9 %copy-start.2 = (f32[2,2,7,64,128]{4,3,2,1,0:T(8,128)}, f32[2,2,7,64,128]{4,3,2,1,0:T(8,128)S(1)}, u32[]{:S(2)}) copy-start(f32[2,2,7,64,128]{4,3,2,1,0:T(8,128)S(1)} %collective-permute-done.1.near_ref) | copy-start | bytes 2752516
  30.6 0.7 %copy-start.3 = (f32[2,2,3,64,128]{4,3,2,1,0:T(8,128)}, f32[2,2,3,64,128]{4,3,2,1,0:T(8,128)S(1)}, u32[]{:S(2)}) copy-start(f32[2,2,3,64,128]{4,3,2,1,0:T(8,128)S(1)} %collective-permute-done.far_ref) | copy-start | bytes 1179652
  35.6 21.5 %collective-permute-start.2 = (f32[2,2,3,64,128]{4,3,2,1,0:T(8,128)}, f32[2,2,3,64,128]{4,3,2,1,0:T(8,128)S(1)}, u32[]{:S(2)}, u32[]{:S(2)}) collective-permute-start(f32[2,2,3,64,128]{4,3,2,1,0:T(8,128)} %get-tuple-element.26), channel_id=1, source_target_pairs={{1,2},{2,1},{3,4},{4,3},{5,6},{6,5},{7,8},{8,7},{9,10},{10,9},{11,... | collective-permute-start | bytes 1179656 | tf_op jit(solution)/shard_map/ppermute | solution.py:538
  42.9 12.2 %copy-start = (f32[2,4,4,64,128]{4,3,2,1,0:T(8,128)S(1)}, f32[2,4,4,64,128]{4,3,2,1,0:T(8,128)}, u32[]{:S(2)}) copy-start(f32[2,4,4,64,128]{4,3,2,1,0:T(8,128)} %get-tuple-element.24.f_ref) | copy-start | bytes 3145732
  42.9 27.4 %all-to-all-start.1 = ((f32[8,2,6,32,128]{4,3,2,1,0:T(8,128)}), f32[8,2,6,32,128]{4,3,2,1,0:T(8,128)S(1)}, u32[]{:S(2)}, u32[]{:S(2)}) async-start(f32[8,2,6,32,128]{4,3,2,1,0:T(8,128)} %bitcast.4), calls=%async_computation.1 | async-start | bytes 3145728 | tf_op jit(solution)/shard_map/all_to_all | solution.py:542
  55.1 1.2 %copy-start.1 = (f32[2,4,4,64,128]{4,3,2,1,0:T(8,128)S(1)}, f32[2,4,4,64,128]{4,3,2,1,0:T(8,128)}, u32[]{:S(2)}) copy-start(f32[2,4,4,64,128]{4,3,2,1,0:T(8,128)} %get-tuple-element.25.a_ref) | copy-start | bytes 3145732
